TPU v7x, 32 devices: a whole 2x2x4 slice. The times are simulated.
32 devices in a mesh: row: 16 (over z, x, core), off: 2 (over y).
Axes of the slice: x: 2, y: 2, z: 4, core: 2. Of those that a mesh axis runs over, the one named last changes fastest.
Arguments:
- vectors: float32 [64, 16384], P(None, 'row'), may hold values from -6 to 6
- tiles: float32 [16384, 4096], P('row', 'off'), may hold values from -0.0625 to 0.0625
- live: int32 [16, 4], P('row', 'off'), may hold values from 256 to 1024
- energies: float32 [16384], P('row'), may hold values from 0.25 to 5.25
- precond: float32 [16384], P('row'), may hold values from 0.03 to 0.3
Outputs:
- basis: float32 [64, 16384], P(None, 'row')
- ritz: float32 [64, 64], replicated
All inputs are finite; a program needn't handle non-finite values.
Results may differ from a plain program's by a relative error of at most 0.00025.
Values sent between devices are 32-bit elements; how exact they have to be, the bound alone decides.
A program may use at most 64 MiB of HBM per device.

v0:
```python
import jax
import jax.numpy as jnp
from jax import lax
from jax.sharding import PartitionSpec as P

ITERS = 2


def from_behind(value, axis, steps):
    count = lax.axis_size(axis)
    pairs = [(source, (source + steps) % count) for source in range(count)]
    return lax.ppermute(value, axis, pairs)


def product(left, right):
    return jnp.dot(left, right, precision=lax.Precision.HIGHEST, preferred_element_type=jnp.float32)


def fetch(vectors, off_index, groups, per_device):
    current = vectors
    travel = vectors
    for target in range(1, groups):
        travel = from_behind(travel, "row", -per_device)
        current = jnp.where(off_index == target, travel, current)
    pieces = [current]
    pieces.append(from_behind(pieces[-1], "row", -1))
    return pieces


def send_back(partials, off_index, groups, per_device):
    gathered = partials[-1]
    gathered = from_behind(gathered, "row", 1) + partials[0]
    carried = jnp.zeros_like(gathered)
    for target in range(groups - 1, 0, -1):
        carried = from_behind(
            carried + jnp.where(off_index == target, gathered, 0.0), "row", per_device
        )
    gathered = carried + jnp.where(off_index == 0, gathered, 0.0)
    return gathered


def apply_ham(vectors, blocks, masks, energies, off_index, groups, per_device):
    pieces = fetch(vectors, off_index, groups, per_device)
    direct = jnp.zeros_like(vectors)
    partials = []
    for slot in range(per_device):
        term = lax.dot_general(
            pieces[slot],
            blocks[slot],
            (((1,), (1,)), ((), ())),
            precision=lax.Precision.HIGHEST,
            preferred_element_type=jnp.float32,
        )
        direct = direct + masks[slot] * term
        partials.append(product(vectors * masks[slot], blocks[slot]))
    returned = send_back(partials, off_index, groups, per_device)
    summed = lax.psum(direct + returned, "off")
    return energies * vectors + summed


def local(vectors, tiles, live, energies, precond):
    width = vectors.shape[1]
    vec_count = vectors.shape[0]
    per_device = tiles.shape[1] // width
    groups = lax.axis_size("off")
    off_index = lax.axis_index("off")
    total_rows = width * lax.axis_size("row")
    row_ids = jnp.arange(width, dtype=jnp.int32)
    masks = [(row_ids < live[0, slot]).astype(jnp.float32) for slot in range(per_device)]
    blocks = [tiles[:, slot * width : (slot + 1) * width] for slot in range(per_device)]
    identity = jnp.eye(vec_count, dtype=jnp.float32)
    ritz_matrix = jnp.zeros((vec_count, vec_count), jnp.float32)
    for iteration in range(ITERS):
        image = apply_ham(vectors, blocks, masks, energies, off_index, groups, per_device)
        weighted_x = precond * vectors
        weighted_y = precond * image
        sums = lax.psum(
            (
                product(vectors, image.T),
                product(vectors, vectors.T),
                product(vectors, weighted_x.T),
                product(vectors, weighted_y.T),
                product(weighted_x, weighted_x.T),
                product(weighted_x, weighted_y.T),
                product(weighted_y, weighted_y.T),
            ),
            "row",
        )
        xy_sum, xx_sum, xpx_sum, xpy_sum, xqx_sum, xqy_sum, yqy_sum = [
            entry / total_rows for entry in sums
        ]
        ritz_matrix = xy_sum
        moved = vectors - precond * (image - product(ritz_matrix.T, vectors))
        correlation = xx_sum - xpy_sum + product(xpx_sum, ritz_matrix) - xpy_sum.T + yqy_sum
        correlation = (
            correlation - product(xqy_sum.T, ritz_matrix) + product(ritz_matrix.T, xpx_sum)
        )
        correlation = (
            correlation
            - product(ritz_matrix.T, xqy_sum)
            + product(product(ritz_matrix.T, xqx_sum), ritz_matrix)
        )
        vectors = product((1.5 * identity - 0.5 * correlation).T, moved)
    return (vectors, ritz_matrix)


def solution(mesh):
    placed = (P(None, "row"), P("row", "off"), P("row", "off"), P("row"), P("row"))
    return jax.shard_map(
        local, mesh=mesh, in_specs=placed, out_specs=(P(None, "row"), P()), check_vma=False
    )
```

profile of v0, /device:TPU:0, one launch (start us, length us, event | category | flops | bytes accessed | tf_op | source)
XLA Modules:
  0.0 348.8 jit_solution(3979965322071925528)
XLA Ops:
  7.2 6.0 %collective-permute-start = (f32[64,1024]{1,0:T(8,128)}, f32[64,1024]{1,0:T(8,128)S(1)}, u32[]{:S(2)}, u32[]{:S(2)}) collective-permute-start(f32[64,1024]{1,0:T(8,128)} %param.5), channel_id=1, source_target_pairs={{0,28},{2,30},{4,0},{6,2},{8,4},{10,6},{12,8},{14,10},{16,12},{18,... | collective-permute-start | bytes 786440 | tf_op jit(solution)/shard_map/ppermute | solution.py:12
  13.2 1.3 fusion.149
  14.6 0.6 fusion.136
  15.2 4.9 %fusion.4 = f32[64,1024]{1,0:T(8,128)S(1)} fusion(f32[1024,2048]{1,0:T(8,128)} %param.6, f32[64,1024]{1,0:T(8,128)} %param.5, f32[1024]{0:T(1024)S(1)} %fusion.136), kind=kOutput, calls=%fused_computation.4 | convolution fusion | flops 805371904 | bytes 4722688 | tf_op jit(solution)/shard_map/dot_general | solution.py:16
  20.1 0.1 collective-permute-start.2
  20.2 2.0 fusion.150
  22.2 0.7 fusion.135
  22.9 1.1 broadcast_select_fusion.3
  24.1 4.5 %collective-permute-start.1 = (f32[64,1024]{1,0:T(8,128)S(1)}, f32[64,1024]{1,0:T(8,128)S(1)}, u32[]{:S(2)}, u32[]{:S(2)}) collective-permute-start(f32[64,1024]{1,0:T(8,128)S(1)} %broadcast_select_fusion.3), channel_id=1, source_target_pairs={{0,30},{2,0},{4,2},{6,4},{8,6},{10,8},{12,10},{14,12},{16,14},{18,... | collective-permute-start | bytes 786440 | tf_op jit(solution)/shard_map/ppermute | solution.py:12
  28.6 0.2 collective-permute-done.2
  28.8 4.9 %broadcast_select_fusion.1 = (f32[64,1024]{1,0:T(8,128)S(1)}, f32[64,1024]{1,0:T(8,128)S(1)}) fusion(pred[]{:T(512)S(6)} %eq.16, f32[64,1024]{1,0:T(8,128)S(1)} %collective-permute-done.2, f32[1024,2048]{1,0:T(8,128)} %param.6, f32[64,1024]{1,0:T(8,128)} %param.5, f32[1024]{0:T(1024)S(1)} %fusion.135), kind=kOutput, calls=%fused_computation.80 | convolution fusion | flops 805502976 | bytes 5246977 | tf_op jit(solution)/shard_map/dot_general | solution.py:16
  33.7 0.1 collective-permute-start.3
  33.8 6.3 %fusion.40 = f32[64,1024]{1,0:T(8,128)S(1)} fusion(f32[64,1024]{1,0:T(8,128)S(1)} %collective-permute-done.1, f32[1024,2048]{1,0:T(8,128)} %param.6, f32[1024]{0:T(1024)S(1)} %fusion.136), kind=kOutput, calls=%fused_computation.24 | convolution fusion | flops 805371904 | bytes 4722688 | tf_op jit(solution)/shard_map/dot_general | solution.py:47
  40.1 2.8 collective-permute-done.3
  42.9 4.9 %fusion.22 = f32[64,1024]{1,0:T(8,128)} fusion(f32[64,1024]{1,0:T(8,128)S(1)} %fusion.40, f32[64,1024]{1,0:T(8,128)S(1)} %broadcast_select_fusion.3, f32[1024,2048]{1,0:T(8,128)S(1)} %copy-done, f32[64,1024]{1,0:T(8,128)S(1)} %collective-permute-done.3, f32[64,1024]{1,0:T(8,128)S(1)} %get-tuple-element.19, f32[1024]{0:T(1024)S(1)} %fusion.135, pred[]{:T(512)S(6)} %eq.17), kind=kOutput, calls=%fused_computation.18 | convolution fusion | flops 805634048 | bytes 5509121 | tf_op jit(solution)/shard_map/dot_general | solution.py:47
  47.8 0.2 all-reduce.13.cloned.1.call-start
  48.0 1.0 fusion.63
  49.0 1.0 convolution_bitcast_fusion.1
  49.9 19.8 %all-reduce.7.cloned.1.call-done = f32[64,1024]{1,0:T(8,128)} async-done(((f32[64,1024]{1,0:T(8,128)}), f32[64,1024]{1,0:T(8,128)}) %all-reduce.7.cloned.1.call-update) | async-done | bytes 262160 | tf_op jit(solution)/shard_map/psum | solution.py:57
  69.8 2.0 convolution_bitcast_fusion
  71.7 1.9 convolution_bitcast_fusion.2
  73.7 1.9 fusion.65
  75.6 2.0 fusion.78
  77.7 90.2 %all-reduce.13.cloned.1.call-done = (f32[64,64]{1,0:T(8,128)}, f32[64,64]{0,1:T(8,128)}, f32[64,64]{1,0:T(8,128)}, f32[64,64]{1,0:T(8,128)}, f32[64,64]{1,0:T(8,...) async-done(((f32[64,64]{1,0:T(8,128)}, f32[64,64]{0,1:T(8,128)}, f32[64,64]{1,0:T(8,128)}, f32[64,64]{1,0:T(8,128)}, f32[64,64]{1,0:T(8,128)}, /*index=5*/f32[64,64]{1,0:T(8,128)}, ...) | async-done | bytes 114704 | tf_op jit(solution)/shard_map/psum | solution.py:77
  167.9 0.8 broadcast_multiply_fusion
  168.6 0.1 copy.8
  168.7 1.0 fusion.106
  169.7 1.0 fusion.56
  170.7 1.0 convolution_subtract_fusion.5
  171.8 1.0 convolution_add_fusion.4
  172.8 1.0 convolution_subtract_fusion.4
  173.8 0.9 fusion.54
  174.7 1.4 fusion.49
  176.1 0.4 fusion.151
  176.6 4.4 %collective-permute-start.4 = (f32[64,1024]{1,0:T(8,128)S(1)}, f32[64,1024]{1,0:T(8,128)S(1)}, u32[]{:S(2)}, u32[]{:S(2)}) collective-permute-start(f32[64,1024]{1,0:T(8,128)S(1)} %fusion.151), channel_id=1, source_target_pairs={{0,28},{2,30},{4,0},{6,2},{8,4},{10,6},{12,8},{14,10},{16,12},{18,... | collective-permute-start | bytes 786440 | tf_op jit(solution)/shard_map/ppermute | solution.py:12
  181.0 4.8 %fusion = f32[64,1024]{1,0:T(8,128)S(1)} fusion(f32[1024,2048]{1,0:T(8,128)} %param.6, f32[64,1024]{1,0:T(8,128)S(1)} %fusion.151, f32[1024]{0:T(1024)S(1)} %fusion.136), kind=kOutput, calls=%fused_computation | convolution fusion | flops 805371904 | bytes 4722688 | tf_op jit(solution)/shard_map/dot_general | solution.py:16
  185.8 0.1 collective-permute-start.6
  185.9 1.0 fusion.152
  186.9 4.5 %collective-permute-start.5 = (f32[64,1024]{1,0:T(8,128)S(1)}, f32[64,1024]{1,0:T(8,128)S(1)}, u32[]{:S(2)}, u32[]{:S(2)}) collective-permute-start(f32[64,1024]{1,0:T(8,128)S(1)} %broadcast_select_fusion.2), channel_id=1, source_target_pairs={{0,30},{2,0},{4,2},{6,4},{8,6},{10,8},{12,10},{14,12},{16,14},{18,... | collective-permute-start | bytes 786440 | tf_op jit(solution)/shard_map/ppermute | solution.py:12
  191.4 3.1 collective-permute-done.6
  194.5 4.8 %broadcast_select_fusion = (f32[64,1024]{1,0:T(8,128)S(1)}, f32[64,1024]{1,0:T(8,128)S(1)}) fusion(pred[]{:T(512)S(6)} %eq.16, f32[64,1024]{1,0:T(8,128)S(1)} %collective-permute-done.6, f32[1024,2048]{1,0:T(8,128)} %param.6, f32[64,1024]{1,0:T(8,128)S(1)} %fusion.151, f32[1024]{0:T(1024)S(1)} %fusion.135), kind=kOutput, calls=%fused_computation.79 | convolution fusion | flops 805502976 | bytes 5246977 | tf_op jit(solution)/shard_map/dot_general | solution.py:16
  199.3 0.3 collective-permute-start.7
  199.6 6.3 %fusion.43 = f32[64,1024]{1,0:T(8,128)S(1)} fusion(f32[64,1024]{1,0:T(8,128)S(1)} %collective-permute-done.5, f32[1024,2048]{1,0:T(8,128)} %param.6, f32[1024]{0:T(1024)S(1)} %fusion.136), kind=kOutput, calls=%fused_computation.25 | convolution fusion | flops 805371904 | bytes 4722688 | tf_op jit(solution)/shard_map/dot_general | solution.py:47
  205.9 2.8 collective-permute-done.7
  208.6 4.9 %fusion.34 = f32[64,1024]{1,0:T(8,128)} fusion(f32[64,1024]{1,0:T(8,128)S(1)} %fusion.43, f32[64,1024]{1,0:T(8,128)S(1)} %broadcast_select_fusion.2, f32[1024,2048]{1,0:T(8,128)S(1)} %bitcast.42, f32[64,1024]{1,0:T(8,128)S(1)} %collective-permute-done.7, f32[64,1024]{1,0:T(8,128)S(1)} %get-tuple-element.21, f32[1024]{0:T(1024)S(1)} %fusion.135, pred[]{:T(512)S(6)} %eq.17), kind=kOutput, calls=%fused_computation.22 | convolution fusion | flops 805634048 | bytes 5509121 | tf_op jit(solution)/shard_map/dot_general | solution.py:47
  213.6 1.0 fusion.57
  214.6 1.0 fusion.61
  215.5 20.0 %all-reduce.9.cloned.1.call-done = f32[64,1024]{1,0:T(8,128)} async-done(((f32[64,1024]{1,0:T(8,128)}), f32[64,1024]{1,0:T(8,128)}) %all-reduce.9.cloned.1.call-update) | async-done | bytes 262160 | tf_op jit(solution)/shard_map/psum | solution.py:57
  235.5 1.9 fusion.59
  237.5 2.0 fusion.73
  239.5 1.9 fusion.75
  241.4 1.9 fusion.81
  243.4 90.2 %all-reduce.11.cloned.1.call-done = (f32[64,64]{1,0:T(8,128)}, f32[64,64]{1,0:T(8,128)}, f32[64,64]{0,1:T(8,128)}, f32[64,64]{1,0:T(8,128)}, f32[64,64]{1,0:T(8,...) async-done(((f32[64,64]{1,0:T(8,128)}, f32[64,64]{1,0:T(8,128)}, f32[64,64]{0,1:T(8,128)}, f32[64,64]{1,0:T(8,128)}, f32[64,64]{1,0:T(8,128)}, /*index=5*/f32[64,64]{1,0:T(8,128)}, ...) | async-done | bytes 114704 | tf_op jit(solution)/shard_map/psum | solution.py:77
  333.6 0.8 broadcast_multiply_fusion.1
  334.4 0.1 copy.12
  334.4 1.0 fusion.104
  335.4 1.0 fusion.52
  336.5 0.1 copy.13
  336.6 1.0 convolution_subtract_fusion.3
  337.6 1.0 convolution_add_fusion.1
  338.6 1.0 convolution_subtract_fusion.2
  339.6 0.2 fusion.51
  339.8 1.4 fusion.47
  341.1 1.1 fusion.153
  (27 shorter events, 0.3 us)
Async XLA Ops:
  7.2 62.6 %all-reduce.7.cloned.1.call-start = ((), (), s32[]{:S(2)}) async-start(), calls=%async_computation | async-start | bytes 524288 | tf_op jit(solution)/shard_map/psum | solution.py:57
  7.2 15.7 %collective-permute-start = (f32[64,1024]{1,0:T(8,128)}, f32[64,1024]{1,0:T(8,128)S(1)}, u32[]{:S(2)}, u32[]{:S(2)}) collective-permute-start(f32[64,1024]{1,0:T(8,128)} %param.5), channel_id=1, source_target_pairs={{0,28},{2,30},{4,0},{6,2},{8,4},{10,6},{12,8},{14,10},{16,12},{18,... | collective-permute-start | bytes 786440 | tf_op jit(solution)/shard_map/ppermute | solution.py:12
  20.1 8.7 %collective-permute-start.2 = (f32[64,1024]{1,0:T(8,128)S(1)}, f32[64,1024]{1,0:T(8,128)S(1)}, u32[]{:S(2)}, u32[]{:S(2)}) collective-permute-start(f32[64,1024]{1,0:T(8,128)S(1)} %fusion.4), channel_id=1, source_target_pairs={{0,2},{2,4},{4,6},{6,8},{8,10},{10,12},{12,14},{14,16},{16,18},{18... | collective-permute-start | bytes 786440 | tf_op jit(solution)/shard_map/ppermute | solution.py:12
  22.2 25.8 %copy-start.1 = (f32[64,1024]{1,0:T(8,128)S(1)}, f32[64,1024]{1,0:T(8,128)}, u32[]{:S(2)}) copy-start(f32[64,1024]{1,0:T(8,128)} %param.5) | copy-start | bytes 786436
  22.2 25.8 %copy-start.3 = (f32[1024]{0:T(1024)S(1)}, f32[1024]{0:T(1024)}, u32[]{:S(2)}) copy-start(f32[1024]{0:T(1024)} %param.9) | copy-start | bytes 12292
  22.9 19.9 %copy-start = (f32[1024,2048]{1,0:T(8,128)S(1)}, f32[1024,2048]{1,0:T(8,128)}, u32[]{:S(2)}) copy-start(f32[1024,2048]{1,0:T(8,128)} %param.6) | copy-start | bytes 25165828
  24.1 45.7 %copy-start.4 = (f32[1024]{0:T(1024)S(1)}, f32[1024]{0:T(1024)}, u32[]{:S(2)}) copy-start(f32[1024]{0:T(1024)} %param.8) | copy-start | bytes 12292
  24.1 9.7 %collective-permute-start.1 = (f32[64,1024]{1,0:T(8,128)S(1)}, f32[64,1024]{1,0:T(8,128)S(1)}, u32[]{:S(2)}, u32[]{:S(2)}) collective-permute-start(f32[64,1024]{1,0:T(8,128)S(1)} %broadcast_select_fusion.3), channel_id=1, source_target_pairs={{0,30},{2,0},{4,2},{6,4},{8,6},{10,8},{12,10},{14,12},{16,14},{18,... | collective-permute-start | bytes 786440 | tf_op jit(solution)/shard_map/ppermute | solution.py:12
  33.7 9.1 %collective-permute-start.3 = (f32[64,1024]{1,0:T(8,128)S(1)}, f32[64,1024]{1,0:T(8,128)S(1)}, u32[]{:S(2)}, u32[]{:S(2)}) collective-permute-start(f32[64,1024]{1,0:T(8,128)S(1)} %get-tuple-element.18), channel_id=1, source_target_pairs={{0,4},{2,6},{4,8},{6,10},{8,12},{10,14},{12,16},{14,18},{16,20},{1... | collective-permute-start | bytes 786440 | tf_op jit(solution)/shard_map/ppermute | solution.py:12
  47.8 120.1 %all-reduce.13.cloned.1.call-start = ((), (), s32[]{:S(2)}) async-start(), calls=%async_computation.3 | async-start | bytes 458752 | tf_op jit(solution)/shard_map/psum | solution.py:77
  77.7 157.8 %all-reduce.9.cloned.1.call-start = ((), (), s32[]{:S(2)}) async-start(), calls=%async_computation.1 | async-start | bytes 524288 | tf_op jit(solution)/shard_map/psum | solution.py:57
  176.1 32.5 %slice-start = ((s8[8388608]{0:T(1024)(128)(4,1)}), s8[4194304]{0:T(1024)(128)(4,1)S(1)}, s32[]{:S(2)}) async-start(s8[8388608]{0:T(1024)(128)(4,1)} %bitcast.41), calls=%async_computation.4 | async-start | bytes 8388608
  176.6 10.3 %collective-permute-start.4 = (f32[64,1024]{1,0:T(8,128)S(1)}, f32[64,1024]{1,0:T(8,128)S(1)}, u32[]{:S(2)}, u32[]{:S(2)}) collective-permute-start(f32[64,1024]{1,0:T(8,128)S(1)} %fusion.151), channel_id=1, source_target_pairs={{0,28},{2,30},{4,0},{6,2},{8,4},{10,6},{12,8},{14,10},{16,12},{18,... | collective-permute-start | bytes 786440 | tf_op jit(solution)/shard_map/ppermute | solution.py:12
  185.8 8.7 %collective-permute-start.6 = (f32[64,1024]{1,0:T(8,128)S(1)}, f32[64,1024]{1,0:T(8,128)S(1)}, u32[]{:S(2)}, u32[]{:S(2)}) collective-permute-start(f32[64,1024]{1,0:T(8,128)S(1)} %fusion), channel_id=1, source_target_pairs={{0,2},{2,4},{4,6},{6,8},{8,10},{10,12},{12,14},{14,16},{16,18},{18... | collective-permute-start | bytes 786440 | tf_op jit(solution)/shard_map/ppermute | solution.py:12
  186.9 21.8 %slice-start.1 = ((s8[8388608]{0:T(1024)(128)(4,1)}), s8[4194304]{0:T(1024)(128)(4,1)S(1)}, s32[]{:S(2)}) async-start(s8[8388608]{0:T(1024)(128)(4,1)} %bitcast.41), calls=%async_computation.5 | async-start | bytes 8388608
  186.9 12.7 %collective-permute-start.5 = (f32[64,1024]{1,0:T(8,128)S(1)}, f32[64,1024]{1,0:T(8,128)S(1)}, u32[]{:S(2)}, u32[]{:S(2)}) collective-permute-start(f32[64,1024]{1,0:T(8,128)S(1)} %broadcast_select_fusion.2), channel_id=1, source_target_pairs={{0,30},{2,0},{4,2},{6,4},{8,6},{10,8},{12,10},{14,12},{16,14},{18,... | collective-permute-start | bytes 786440 | tf_op jit(solution)/shard_map/ppermute | solution.py:12
  199.3 9.3 %collective-permute-start.7 = (f32[64,1024]{1,0:T(8,128)S(1)}, f32[64,1024]{1,0:T(8,128)S(1)}, u32[]{:S(2)}, u32[]{:S(2)}) collective-permute-start(f32[64,1024]{1,0:T(8,128)S(1)} %get-tuple-element.20), channel_id=1, source_target_pairs={{0,4},{2,6},{4,8},{6,10},{8,12},{10,14},{12,16},{14,18},{16,20},{1... | collective-permute-start | bytes 786440 | tf_op jit(solution)/shard_map/ppermute | solution.py:12
  213.6 120.0 %all-reduce.11.cloned.1.call-start = ((), (), s32[]{:S(2)}) async-start(), calls=%async_computation.2 | async-start | bytes 458752 | tf_op jit(solution)/shard_map/psum | solution.py:77
  334.4 7.9 %copy-start.2 = (f32[64,64]{1,0:T(8,128)}, f32[64,64]{1,0:T(8,128)S(1)}, u32[]{:S(2)}) copy-start(f32[64,64]{1,0:T(8,128)S(1)} %get-tuple-element.22) | copy-start | bytes 49156
Sparse Core Ops, SparseCore 0:
  47.9 21.8 all-reduce.6
  77.8 90.0 all-reduce.12
  213.7 21.7 all-reduce.8
  243.5 90.0 all-reduce.10
where the time goes:
time: 351 us; the launch traced here: 349 us
  waiting for transfers between devices  229 us (65%)
  matrix products  79.8 us (23%)
  starting transfers between devices  20.2 us (6%)
  between operations  14.1 us (4%)
  other arithmetic  4.06 us (1%)
    psum x2, waiting for transfers between devices, local(): lax.psum((product(vectors, image.T), product(vectors, vectors.T), product...  180 us
    dot_general x34, matrix products, product(): jnp.dot(left, right, precision=lax.Precision.HIGHEST, preferred_element_t...  57.6 us
    psum x2, waiting for transfers between devices, apply_ham(): summed = lax.psum(direct + returned, 'off')  39.8 us
    dot_general x4, matrix products, apply_ham(): lax.dot_general(pieces[slot], blocks[slot], (((1,), (1,)), ((), ())), pre...  22.3 us
    ppermute x8, starting transfers between devices, from_behind(): return lax.ppermute(value, axis, pairs)  19.8 us
    ppermute x8, waiting for transfers between devices, from_behind(): return lax.ppermute(value, axis, pairs)  8.88 us
  transfers between devices with their start and end apart: 12, of which 8 were waited for; matrix products, arithmetic and copies ran while one was open for 12% of the time, Pallas kernels for 0%

commit v1 on v0

v1 whole, which is shorter than its diff:
```python
import functools

import jax
import jax.numpy as jnp
from jax import lax
from jax.experimental import pallas as pl
from jax.experimental.pallas import tpu as pltpu
from jax.sharding import PartitionSpec as P

ITERS = 2
MESH = pl.DeviceIdType.MESH
HIGHEST = lax.Precision.HIGHEST
NN = (((1,), (0,)), ((), ()))
NT = (((1,), (1,)), ((), ()))


def exact(left, right, dims=NN):
    return lax.dot_general(
        left, right, dims, precision=HIGHEST, preferred_element_type=jnp.float32
    )


def coarse(left, right, dims):
    return lax.dot_general(left, right, dims, preferred_element_type=jnp.float32)


def halves(value):
    high = value.astype(jnp.bfloat16)
    low = (value - high.astype(jnp.float32)).astype(jnp.bfloat16)
    return high, low


def kernel(
    n, n_off, slots, total_rows,
    vec_ref, tiles_ref, live_ref, energy_ref, precond_ref,
    out_ref, ritz_ref,
    raw, high, low, mine, near, split, direct, back, ret, part_a, own_a, near_a,
    gram, gram_in, gram_off, gram_sum, gram_all,
    load_sem, fetch_send, fetch_recv, ret_send, ret_recv, share_send, share_recv,
    peer_send, peer_recv, gs_send, gs_recv, go_send, go_recv, ga_send, ga_recv,
):
    me = lax.axis_index("row")
    off = lax.axis_index("off")
    k, width = vec_ref.shape
    part = width // n_off
    chunk = min(256, part)
    grow = 2 * k // n

    def copy(src, dst, send, recv, row, col):
        return pltpu.make_async_remote_copy(
            src_ref=src, dst_ref=dst, send_sem=send, recv_sem=recv,
            device_id=(row, col), device_id_type=MESH,
        )

    def row_at(shift):
        return lax.rem(me + shift + n, n)

    def peer(step):
        return lax.rem(off + step, n_off)

    def cols(index):
        return pl.ds(pl.multiple_of(index * part, part), part)

    loads = []
    for slot in range(slots):
        load = pltpu.make_async_copy(
            tiles_ref.at[:, pl.ds(slot * width, width)], raw.at[slot], load_sem.at[slot]
        )
        load.start()
        loads.append(load)

    barrier = pltpu.get_barrier_semaphore()

    def greet(step, carry):
        flat = lax.rem(me * n_off + off + step, n * n_off)
        pl.semaphore_signal(
            barrier, inc=1, device_id=(flat // n_off, lax.rem(flat, n_off)),
            device_id_type=MESH,
        )
        return carry

    lax.fori_loop(1, n * n_off, greet, 0)
    mine[:k, :] = vec_ref[...]
    mine[k:, :] = jnp.broadcast_to(precond_ref[...], (mine.shape[0] - k, width))
    pl.semaphore_wait(barrier, n * n_off - 1)

    def spread(src, dst, send, recv):
        started = []
        for group in range(n_off):
            for slot in range(slots):
                shift = group * slots + slot
                if shift:
                    one = copy(
                        src, dst.at[slot, :, cols(off)], send.at[shift],
                        recv.at[slot, off], row_at(-shift), group,
                    )
                    one.start()
                    started.append(one)
        return started

    def gathered(slot, dst, recv):
        for step in range(n_off):
            where = dst.at[slot, :, cols(step)]
            copy(where, where, recv.at[slot, step], recv.at[slot, step],
                 row_at(1), off).wait_recv()

    sent = spread(mine.at[:, cols(off)], near, fetch_send, fetch_recv)

    def put_split(where, value):
        hi, lo = halves(value)
        split[where, :k, :] = hi
        split[where, k:, :] = lo

    put_split(slots, vec_ref[...])

    def transposed(it, slot):
        shift = off * slots + slot
        for q in range(n_off):
            for c in range(part // chunk):
                at = pl.ds(q * part + c * chunk, chunk)
                both = coarse(split[slots], high[slot, :, at], NN)
                rest = coarse(split[slots, :k, :], low[slot, :, at], NN)
                back[it, slot, q, :, pl.ds(c * chunk, chunk)] = both[:k] + both[k:] + rest

            @pl.when(shift != 0)
            def _():
                copy(
                    back.at[it, slot, q], ret.at[it, off, slot],
                    ret_send.at[it, slot, q], ret_recv.at[it, off, slot],
                    row_at(shift), q,
                ).start()

    def forward(it, slot, first):
        for c in range(width // chunk):
            at = pl.ds(c * chunk, chunk)
            both = coarse(split[slot], high[slot, at, :], NT)
            rest = coarse(split[slot, :k, :], low[slot, at, :], NT)
            term = both[:k] + both[k:] + rest
            q, place = (c * chunk) // part, (c * chunk) % part
            where = pl.ds(place, chunk)
            if first:
                direct[it, q, :, where] = term
            else:
                direct[it, q, :, where] = direct[it, q, :, where] + term

    order = list(range(slots - 1, -1, -1))
    rows = 32
    for slot in order:
        loads[slot].wait()
        limit = live_ref[0, slot]

        def cut(index, carry):
            start = pl.multiple_of(index * rows, rows)
            ids = lax.broadcasted_iota(jnp.int32, (rows, width), 0) + start
            value = jnp.where(ids < limit, raw[slot, pl.ds(start, rows), :], 0.0)
            hi, lo = halves(value)
            high[slot, pl.ds(start, rows), :] = hi
            low[slot, pl.ds(start, rows), :] = lo
            return carry

        lax.fori_loop(0, width // rows, cut, 0)
        transposed(0, slot)

    for slot in order:
        if slot == 0:
            @pl.when(off == 0)
            def _():
                split[0] = split[slots]
                near[0] = mine[...]

            @pl.when(off != 0)
            def _():
                gathered(0, near, fetch_recv)
                put_split(0, near[0, :k, :])
        else:
            gathered(slot, near, fetch_recv)
            put_split(slot, near[slot, :k, :])

    def eye():
        return (
            lax.broadcasted_iota(jnp.int32, (k, k), 0)
            == lax.broadcasted_iota(jnp.int32, (k, k), 1)
        ).astype(jnp.float32)

    state = mine
    for it in range(ITERS):
        last = it == ITERS - 1
        for position, slot in enumerate(order):
            forward(it, slot, position == 0)

        @pl.when(off == 0)
        def _():
            for q in range(n_off):
                direct[it, q] = direct[it, q] + back[it, 0, q]

        for step in range(1, n_off):
            copy(
                direct.at[it, peer(step)], ret.at[it, off, slots],
                ret_send.at[it, slots, step], ret_recv.at[it, off, slots],
                me, peer(step),
            ).start()

        x_part = state[:k, cols(off)]
        p_part = precond_ref[:, cols(off)]
        total = energy_ref[:, cols(off)] * x_part + direct[it, off]
        for group in range(n_off):
            for slot in range(slots):
                if group or slot:
                    where = ret.at[it, group, slot]
                    copy(where, where, ret_send.at[it, 0, 0], ret_recv.at[it, group, slot],
                         row_at(1), off).wait_recv()
                    total = total + ret[it, group, slot]
        for step in range(1, n_off):
            where = ret.at[it, peer(step), slots]
            copy(where, where, ret_send.at[it, 0, 0], ret_recv.at[it, peer(step), slots],
                 row_at(1), off).wait_recv()
            total = total + ret[it, peer(step), slots]

        a_part = x_part - p_part * total
        part_a[it] = a_part
        own_a[it, :, cols(off)] = a_part
        for step in range(1, n_off):
            copy(
                part_a.at[it], own_a.at[it, :, cols(off)],
                peer_send.at[it, step], peer_recv.at[it, off], me, peer(step),
            ).start()
        if not last:
            sent += spread(part_a.at[it], near_a, share_send, share_recv)

        ab = jnp.concatenate([a_part, p_part * x_part], axis=0)
        inner = exact(ab, ab, NT)
        xy = exact(x_part, total, NT)
        low_half = jnp.concatenate([xy, inner[k:, k:]], axis=1)
        packed = jnp.concatenate([inner[:k, :], low_half], axis=0)
        for t in range(n):
            gram[it, t] = packed[t * grow : (t + 1) * grow, :]

        for step in range(1, n):
            target = row_at(step)
            copy(
                gram.at[it, target], gram_in.at[it, me], gs_send.at[it, step],
                gs_recv.at[it, me], target, off,
            ).start()
        piece = gram[it, me]
        for step in range(1, n):
            source = row_at(step)
            where = gram_in.at[it, source]
            copy(where, where, gs_send.at[it, step], gs_recv.at[it, source],
                 row_at(1), off).wait_recv()
            piece = piece + gram_in[it, source]
        gram_off[it, off] = piece
        for step in range(1, n_off):
            copy(
                gram_off.at[it, off], gram_off.at[it, off], go_send.at[it, step],
                go_recv.at[it, off], me, peer(step),
            ).start()
        for step in range(1, n_off):
            where = gram_off.at[it, peer(step)]
            copy(where, where, go_send.at[it, step], go_recv.at[it, peer(step)],
                 row_at(1), off).wait_recv()
        piece = gram_off[it, 0]
        for q in range(1, n_off):
            piece = piece + gram_off[it, q]
        gram_sum[it] = piece
        gram_all[it, me] = piece
        for step in range(1, n):
            copy(
                gram_sum.at[it], gram_all.at[it, me], ga_send.at[it, step],
                ga_recv.at[it, me], row_at(step), off,
            ).start()
        for step in range(1, n):
            source = row_at(step)
            where = gram_all.at[it, source]
            copy(where, where, ga_send.at[it, step], ga_recv.at[it, source],
                 row_at(1), off).wait_recv()
        full = jnp.concatenate([gram_all[it, t] for t in range(n)], axis=0) / total_rows
        turned = full.T
        ritz, ritz_t = full[k:, :k], turned[:k, k:]
        aa, cross, cross_t, bb = full[:k, :k], full[:k, k:], turned[k:, :k], full[k:, k:]
        mixed = exact(cross, ritz)
        overlap = aa + mixed + exact(ritz_t, cross_t + exact(bb, ritz))
        fix = 1.5 * eye() - 0.5 * overlap
        both_fix = jnp.concatenate([fix, exact(fix, ritz_t)], axis=1)

        def update(a_value, x_value, p_row):
            return exact(both_fix, jnp.concatenate([a_value, p_row * x_value], axis=0))

        for step in range(1, n_off):
            where = own_a.at[it, :, cols(peer(step))]
            copy(where, where, peer_send.at[it, step], peer_recv.at[it, peer(step)],
                 row_at(1), off).wait_recv()
        fresh = update(own_a[it], state[:k, :], precond_ref[...])
        out_ref[...] = fresh
        if last:
            ritz_ref[...] = ritz
        else:
            put_split(slots, fresh)
            for slot in order:
                transposed(it + 1, slot)

            def renew(slot):
                gathered(slot, near_a, share_recv)
                value = update(
                    near_a[slot], near[slot, :k, :], near[slot, k : k + 1, :]
                )
                near[slot, :k, :] = value
                put_split(slot, value)

            for slot in order:
                if slot == 0:
                    @pl.when(off == 0)
                    def _():
                        split[0] = split[slots]

                    @pl.when(off != 0)
                    def _():
                        renew(0)
                else:
                    renew(slot)
            state = out_ref

    for one in sent:
        one.wait_send()
    for it in range(ITERS):
        for slot in range(slots):
            for q in range(n_off):
                @pl.when(off * slots + slot != 0)
                def _():
                    copy(back.at[it, slot, q], ret.at[it, off, slot], ret_send.at[it, slot, q],
                         ret_recv.at[it, off, slot], row_at(1), q).wait_send()
        for step in range(1, n_off):
            copy(direct.at[it, 0], ret.at[it, off, slots], ret_send.at[it, slots, step],
                 ret_recv.at[it, off, slots], me, peer(step)).wait_send()
            copy(part_a.at[it], part_a.at[it], peer_send.at[it, step],
                 peer_recv.at[it, off], me, peer(step)).wait_send()
            copy(gram_sum.at[it], gram_sum.at[it], go_send.at[it, step],
                 go_recv.at[it, off], me, peer(step)).wait_send()
        for step in range(1, n):
            copy(gram_sum.at[it], gram_sum.at[it], gs_send.at[it, step],
                 gs_recv.at[it, me], row_at(step), off).wait_send()
            copy(gram_sum.at[it], gram_sum.at[it], ga_send.at[it, step],
                 ga_recv.at[it, me], row_at(step), off).wait_send()


def local(n, n_off, vectors, tiles, live, energies, precond):
    k, width = vectors.shape
    slots = tiles.shape[1] // width
    part = width // n_off
    grow = 2 * k // n
    f32, b16 = jnp.float32, jnp.bfloat16
    vmem, dma = pltpu.VMEM, pltpu.SemaphoreType.DMA
    inside = pl.BlockSpec(memory_space=pltpu.VMEM)
    return pl.pallas_call(
        functools.partial(kernel, n, n_off, slots, float(width * n)),
        out_shape=(
            jax.ShapeDtypeStruct((k, width), f32),
            jax.ShapeDtypeStruct((k, k), f32),
        ),
        in_specs=[
            inside,
            pl.BlockSpec(memory_space=pl.ANY),
            pl.BlockSpec(memory_space=pltpu.SMEM),
            inside,
            inside,
        ],
        out_specs=(inside, inside),
        scratch_shapes=[
            vmem((slots, width, width), f32),
            vmem((slots, width, width), b16),
            vmem((slots, width, width), b16),
            vmem((k + 8, width), f32),
            vmem((slots, k + 8, width), f32),
            vmem((slots + 1, 2 * k, width), b16),
            vmem((ITERS, n_off, k, part), f32),
            vmem((ITERS, slots, n_off, k, part), f32),
            vmem((ITERS, n_off, slots + 1, k, part), f32),
            vmem((ITERS, k, part), f32),
            vmem((ITERS, k, width), f32),
            vmem((slots, k, width), f32),
            vmem((ITERS, n, grow, 2 * k), f32),
            vmem((ITERS, n, grow, 2 * k), f32),
            vmem((ITERS, n_off, grow, 2 * k), f32),
            vmem((ITERS, grow, 2 * k), f32),
            vmem((ITERS, n, grow, 2 * k), f32),
            dma((slots,)),
            dma((n_off * slots,)),
            dma((slots, n_off)),
            dma((ITERS, slots + 1, n_off)),
            dma((ITERS, n_off, slots + 1)),
            dma((n_off * slots,)),
            dma((slots, n_off)),
            dma((ITERS, n_off)),
            dma((ITERS, n_off)),
            dma((ITERS, n)),
            dma((ITERS, n)),
            dma((ITERS, n_off)),
            dma((ITERS, n_off)),
            dma((ITERS, n)),
            dma((ITERS, n)),
        ],
        compiler_params=pltpu.CompilerParams(
            collective_id=0, has_side_effects=True, vmem_limit_bytes=48 * 1024 * 1024
        ),
    )(vectors, tiles, live, energies[None, :], precond[None, :])


def solution(mesh):
    placed = (P(None, "row"), P("row", "off"), P("row", "off"), P("row"), P("row"))
    return jax.shard_map(
        functools.partial(local, mesh.shape["row"], mesh.shape["off"]),
        mesh=mesh, in_specs=placed, out_specs=(P(None, "row"), P()), check_vma=False,
    )
```

time: 351 us -> 82.7 us (0.24)
  waiting for transfers between devices: 229 us -> 0 us
  matrix products: 79.8 us -> 0 us
  Pallas kernels: 0 us -> 77.6 us
  starting transfers between devices: 20.2 us -> 0 us
  between operations: 14.1 us -> 0.65 us
  other arithmetic: 4.06 us -> 0 us
    psum x4 -> x0, waiting for transfers between devices: 220 us -> none  [the longest x2 180 us: local(): lax.psum((product(vectors, image.T), product(vectors, vectors.T), product...]
    dot_general x38 -> x0, matrix products: 79.8 us -> none  [the longest x34 57.6 us: product(): jnp.dot(left, right, precision=lax.Precision.HIGHEST, preferred_element_t...]
    pallas_call x0 -> x1, Pallas kernels: none -> 77.6 us  [local(): pl.pallas_call(functools.partial(kernel, n, n_off, slots, float(width * n...]
    ppermute x8 -> x0, starting transfers between devices: 19.8 us -> none  [from_behind(): return lax.ppermute(value, axis, pairs)]
    ppermute x8 -> x0, waiting for transfers between devices: 8.88 us -> none  [from_behind(): return lax.ppermute(value, axis, pairs)]
    unnamed x14 -> x10, local copies, waits for them, and re-layouts: 0.04 us -> 4.29 us
  transfers between devices with their start and end apart: 12 -> 0, of which waited for: 8 -> 0; matrix products, arithmetic and copies ran while one was open for 12% -> 0% of each run, Pallas kernels for 0% -> 0%
where the time goes in v1:
time: 82.7 us; the launch traced here: 82.5 us
  Pallas kernels  77.6 us (94%)
  local copies, waits for them, and re-layouts  4.29 us (5%)
    pallas_call x1, Pallas kernels, local(): pl.pallas_call(functools.partial(kernel, n, n_off, slots, float(width * n...  77.6 us
    unnamed x10, local copies, waits for them, and re-layouts  4.29 us

profile of v1, /device:TPU:0, one launch (start us, length us, event | category | flops | bytes accessed | tf_op | source)
XLA Modules:
  0.0 82.5 jit_solution(7991153234233603239)
XLA Ops:
  0.6 0.0 copy-start
  0.6 0.9 %copy-done = f32[64,1024]{1,0:T(8,128)S(1)} copy-done((f32[64,1024]{1,0:T(8,128)S(1)}, f32[64,1024]{1,0:T(8,128)}, u32[]{:S(2)}) %copy-start) | copy-done | bytes 262168
  1.6 0.0 copy-start.1
  1.6 0.7 copy-done.1
  2.3 0.0 copy-start.2
  2.3 0.7 copy-done.2
  3.0 0.0 copy-start.3
  3.0 0.7 copy-done.3
  3.6 77.6 %shard_map.68 = (f32[64,1024]{1,0:T(8,128)S(1)}, f32[64,64]{1,0:T(8,128)S(1)}) custom-call(f32[64,1024]{1,0:T(8,128)S(1)} %copy-done, f32[1024,2048]{1,0:T(8,128)} %tiles_ref.1, s32[1,2]{1,0:T(1,128)S(1)} %copy-done.3, f32[1,1024]{1,0:T(1,128)S(1)} %bitcast.2, f32[1,1024]{1,0:T(1,128)S(1)} %bitcast.3), custom_call_target="tpu_custom_call" | custom-call | tf_op jit(solution)/shard_map/pallas_call | solution.py:353
  81.2 0.7 copy.9
  81.9 0.6 copy.10
Async XLA Ops:
  0.6 1.0 %copy-start = (f32[64,1024]{1,0:T(8,128)S(1)}, f32[64,1024]{1,0:T(8,128)}, u32[]{:S(2)}) copy-start(f32[64,1024]{1,0:T(8,128)} %vec_ref.1) | copy-start | bytes 786436
  1.6 0.7 copy-start.1
  2.3 0.7 copy-start.2
  3.0 0.7 copy-start.3

commit v2 on v1

v2 whole, which is shorter than its diff:
```python
import functools

import jax
import jax.numpy as jnp
from jax import lax
from jax.experimental import pallas as pl
from jax.experimental.pallas import tpu as pltpu
from jax.sharding import PartitionSpec as P

ITERS = 2
MESH = pl.DeviceIdType.MESH
NN = (((1,), (0,)), ((), ()))
NT = (((1,), (1,)), ((), ()))


def coarse(left, right, dims):
    return lax.dot_general(left, right, dims, preferred_element_type=jnp.float32)


def halves(value):
    high = value.astype(jnp.bfloat16)
    low = (value - high.astype(jnp.float32)).astype(jnp.bfloat16)
    return high, low


def triple(left, right, dims=NN):
    left_hi, left_lo = halves(left)
    right_hi, right_lo = halves(right)
    count = left.shape[0]
    both = coarse(jnp.concatenate([left_hi, left_lo], axis=0), right_hi, dims)
    return both[:count] + both[count:] + coarse(left_hi, right_lo, dims)


def kernel(
    n, n_off, slots, total_rows,
    vec_hbm, tiles_ref, live_hbm, energy_hbm, precond_hbm,
    out_ref, ritz_ref,
    vec_ref, live_ref, energy_ref, precond_ref, acc, hand,
    raw, high, low, mine, near, split, direct, back, ret, part_a, own_a, near_a,
    gram, gram_in, gram_sum, gram_all,
    load_sem, hand_recv, fetch_relay, share_relay, fetch_send, fetch_recv, ret_send, ret_recv, share_send, share_recv,
    peer_send, peer_recv, gs_send, gs_recv, ga_send, ga_recv,
):
    me = lax.axis_index("row")
    off = lax.axis_index("off")
    k, width = vec_ref.shape
    part = width // n_off
    chunk = min(256, part)
    owners = min(n_off, 2 * k // n)
    grow = 2 * k // (n * owners)
    devices = n * n_off
    flat_me = me * n_off + off
    odd = lax.rem(me, 2) == 1
    small = devices <= 32

    def copy(src, dst, send, recv, row, col):
        return pltpu.make_async_remote_copy(
            src_ref=src, dst_ref=dst, send_sem=send, recv_sem=recv,
            device_id=(row, col), device_id_type=MESH,
        )

    def row_at(shift):
        return lax.rem(me + shift + n, n)

    def peer(step):
        return lax.rem(off + step, n_off)

    def cols(index):
        return pl.ds(pl.multiple_of(index * part, part), part)

    heads = [
        pltpu.make_async_copy(src, dst, load_sem.at[slots + index])
        for index, (src, dst) in enumerate(
            ((vec_hbm, vec_ref), (precond_hbm, precond_ref),
             (energy_hbm, energy_ref), (live_hbm, live_ref))
        )
    ]
    for one in heads:
        one.start()
    order = list(range(slots - 1, -1, -1))
    loads = [
        pltpu.make_async_copy(
            tiles_ref.at[:, pl.ds(slot * width, width)], raw.at[slot], load_sem.at[slot]
        )
        for slot in range(slots)
    ]
    for slot in order:
        loads[slot].start()

    barrier = pltpu.get_barrier_semaphore()

    def greet(step, carry):
        flat = lax.rem(flat_me + step, devices)
        pl.semaphore_signal(
            barrier, inc=1, device_id=(flat // n_off, lax.rem(flat, n_off)),
            device_id_type=MESH,
        )
        return carry

    lax.fori_loop(1, devices, greet, 0, unroll=small)
    for one in heads:
        one.wait()
    mine[:k, :] = vec_ref[...]
    mine[k:, :] = jnp.broadcast_to(precond_ref[...], (mine.shape[0] - k, width))
    pl.semaphore_wait(barrier, devices - 1)

    def spread(src, dst, send, recv, act):
        for group in range(n_off):
            for slot in range(slots):
                shift = group * slots + slot

                def step():
                    one = copy(
                        src, dst.at[slot, :, cols(off)], send.at[shift],
                        recv.at[slot, off], row_at(-shift), group,
                    )
                    act(one)

                if slot:
                    pl.when(lax.rem(me + shift, 2) == 1)(step)
                elif shift:
                    step()

    def relay(dst, send, recv, act):
        @pl.when(odd)
        def _():
            for slot in range(slots - 1):
                for q in range(n_off):
                    act(copy(
                        dst.at[slot, :, cols(q)], dst.at[slot + 1, :, cols(q)],
                        send.at[slot, q], recv.at[slot + 1, q], row_at(-1), off,
                    ))

    def begin(one):
        one.start()

    def finish(one):
        one.wait_send()

    def gathered(slot, dst, recv):
        for step in range(n_off):
            where = dst.at[slot, :, cols(step)]
            copy(where, where, recv.at[slot, step], recv.at[slot, step],
                 row_at(1), off).wait_recv()

    spread(mine.at[:, cols(off)], near, fetch_send, fetch_recv, begin)

    def put_split(where, value):
        hi, lo = halves(value)
        split[where, :k, :] = hi
        split[where, k:, :] = lo

    put_split(slots, vec_ref[...])

    def transposed(it, slot):
        shift = off * slots + slot
        for q in range(n_off):
            for c in range(part // chunk):
                at = pl.ds(q * part + c * chunk, chunk)
                both = coarse(split[slots], high[slot, :, at], NN)
                rest = coarse(split[slots, :k, :], low[slot, :, at], NN)
                back[it, slot, q, :, pl.ds(c * chunk, chunk)] = both[:k] + both[k:] + rest

            if slot < slots - 1:
                @pl.when(odd)
                def _():
                    where = hand.at[it, slot, q]
                    copy(where, where, hand_recv.at[it, slot, q], hand_recv.at[it, slot, q],
                         row_at(1), off).wait_recv()
                    back[it, slot, q] = back[it, slot, q] + hand[it, slot, q]

            def away():
                copy(
                    back.at[it, slot, q], ret.at[it, off, slot],
                    ret_send.at[it, slot, q], ret_recv.at[it, off, slot],
                    row_at(shift), q,
                ).start()

            if slot:
                pl.when(odd)(away)

                @pl.when(jnp.logical_not(odd))
                def _():
                    copy(
                        back.at[it, slot, q], hand.at[it, slot - 1, q],
                        ret_send.at[it, slot, q], hand_recv.at[it, slot - 1, q],
                        row_at(1), off,
                    ).start()
            else:
                pl.when(shift != 0)(away)

    def forward(it, slot, first):
        for c in range(width // chunk):
            at = pl.ds(c * chunk, chunk)
            both = coarse(split[slot], high[slot, at, :], NT)
            rest = coarse(split[slot, :k, :], low[slot, at, :], NT)
            term = both[:k] + both[k:] + rest
            q, place = (c * chunk) // part, (c * chunk) % part
            where = pl.ds(place, chunk)
            if first:
                direct[it, q, :, where] = term
            else:
                direct[it, q, :, where] = direct[it, q, :, where] + term

    rows = 32
    for slot in order:
        loads[slot].wait()
        limit = live_ref[0, slot]

        def cut(index, carry):
            start = pl.multiple_of(index * rows, rows)
            ids = lax.broadcasted_iota(jnp.int32, (rows, width), 0) + start
            value = jnp.where(ids < limit, raw[slot, pl.ds(start, rows), :], 0.0)
            hi, lo = halves(value)
            high[slot, pl.ds(start, rows), :] = hi
            low[slot, pl.ds(start, rows), :] = lo
            return carry

        lax.fori_loop(0, width // rows, cut, 0)
        transposed(0, slot)

    def collect(dst, own, send, recv, use):
        for slot in range(slots):
            if slot == 0:
                @pl.when(off == 0)
                def _():
                    dst[0] = own[...]

                @pl.when(off != 0)
                def _():
                    gathered(0, dst, recv)
            else:
                gathered(slot, dst, recv)
            if slot == slots - 2:
                relay(dst, send, recv, begin)
            use(slot)

    def eye():
        return (
            lax.broadcasted_iota(jnp.int32, (k, k), 0)
            == lax.broadcasted_iota(jnp.int32, (k, k), 1)
        ).astype(jnp.float32)

    state = mine
    for it in range(ITERS):
        last = it == ITERS - 1
        if it == 0:
            def use(slot):
                put_split(slot, near[slot, :k, :])
                forward(0, slot, slot == 0)

            collect(near, mine, fetch_relay, fetch_recv, use)

        @pl.when(off == 0)
        def _():
            for q in range(n_off):
                direct[it, q] = direct[it, q] + back[it, 0, q]

        for step in range(1, n_off):
            copy(
                direct.at[it, peer(step)], ret.at[it, off, slots],
                ret_send.at[it, slots, step], ret_recv.at[it, off, slots],
                me, peer(step),
            ).start()

        x_part = state[:k, cols(off)]
        p_part = precond_ref[:, cols(off)]
        acc[...] = energy_ref[:, cols(off)] * x_part + direct[it, off]
        for group in range(n_off):
            for slot in range(slots):
                def take():
                    where = ret.at[it, group, slot]
                    copy(where, where, ret_send.at[it, 0, 0], ret_recv.at[it, group, slot],
                         row_at(1), off).wait_recv()
                    acc[...] = acc[...] + ret[it, group, slot]

                if slot:
                    pl.when(lax.rem(me + group * slots + slot, 2) == 1)(take)
                elif group:
                    take()
        total = acc[...]
        for step in range(1, n_off):
            where = ret.at[it, peer(step), slots]
            copy(where, where, ret_send.at[it, 0, 0], ret_recv.at[it, peer(step), slots],
                 row_at(1), off).wait_recv()
            total = total + ret[it, peer(step), slots]

        a_part = x_part - p_part * total
        part_a[it] = a_part
        own_a[it, :, cols(off)] = a_part
        for step in range(1, n_off):
            copy(
                part_a.at[it], own_a.at[it, :, cols(off)],
                peer_send.at[it, step], peer_recv.at[it, off], me, peer(step),
            ).start()
        if not last:
            spread(part_a.at[it], near_a, share_send, share_recv, begin)

        ab = jnp.concatenate([a_part, p_part * x_part], axis=0)
        inner = triple(ab, ab, NT)
        xy = triple(x_part, total, NT)
        low_half = jnp.concatenate([xy, inner[k:, k:]], axis=1)
        packed = jnp.concatenate([inner[:k, :], low_half], axis=0)
        for t in range(n * owners):
            gram[it, t] = packed[t * grow : (t + 1) * grow, :]

        def owner_at(step):
            index = lax.rem(me * owners + lax.rem(off, owners) + step, n * owners)
            return index, index // owners, lax.rem(index, owners)

        def deal(step, carry):
            index, row, col = owner_at(step)
            copy(
                gram.at[it, index], gram_in.at[it, flat_me], gs_send.at[it, index],
                gs_recv.at[it, flat_me], row, col,
            ).start()
            return carry

        def add(step, piece):
            source = lax.rem(flat_me + step, devices)
            where = gram_in.at[it, source]
            copy(where, where, gs_send.at[it, 0], gs_recv.at[it, source],
                 row_at(1), off).wait_recv()
            return piece + gram_in[it, source]

        def tell(step, carry):
            target = lax.rem(flat_me + step, devices)
            copy(
                gram_sum.at[it], gram_all.at[it, me * owners + off], ga_send.at[it, target],
                ga_recv.at[it, me * owners + off], target // n_off, lax.rem(target, n_off),
            ).start()
            return carry

        def hear(step, carry):
            index = owner_at(step)[0]
            where = gram_all.at[it, index]
            copy(where, where, ga_send.at[it, 0], ga_recv.at[it, index],
                 row_at(1), off).wait_recv()
            return carry

        def own():
            piece = lax.fori_loop(
                1, devices, add, gram[it, me * owners + off], unroll=small
            )
            gram_sum[it] = piece
            gram_all[it, me * owners + off] = piece
            lax.fori_loop(1, devices, tell, 0, unroll=small)

        lax.fori_loop(1, n * owners, deal, 0, unroll=small)
        if owners == n_off:
            own()
        else:
            pl.when(off < owners)(own)

            @pl.when(off >= owners)
            def _():
                deal(0, 0)
                hear(0, 0)

        lax.fori_loop(1, n * owners, hear, 0, unroll=small)
        full = gram_all[it].reshape(2 * k, 2 * k) / total_rows
        turned = full.T
        ritz, ritz_t = full[k:, :k], turned[:k, k:]
        aa, cross, cross_t, bb = full[:k, :k], full[:k, k:], turned[k:, :k], full[k:, k:]
        mixed = triple(jnp.concatenate([cross, bb], axis=0), ritz)
        overlap = aa + mixed[:k] + triple(ritz_t, cross_t + mixed[k:])
        fix = 1.5 * eye() - 0.5 * overlap
        both_fix = jnp.concatenate([fix, triple(fix, ritz_t)], axis=1)

        def update(a_value, x_value, p_row):
            return triple(both_fix, jnp.concatenate([a_value, p_row * x_value], axis=0))

        for step in range(1, n_off):
            where = own_a.at[it, :, cols(peer(step))]
            copy(where, where, peer_send.at[it, step], peer_recv.at[it, peer(step)],
                 row_at(1), off).wait_recv()
        fresh = update(own_a[it], state[:k, :], precond_ref[...])
        out_ref[...] = fresh
        if last:
            ritz_ref[...] = ritz
        else:
            put_split(slots, fresh)
            for slot in order:
                transposed(it + 1, slot)

            def renew(slot):
                value = update(
                    near_a[slot], near[slot, :k, :], near[slot, k : k + 1, :]
                )
                put_split(slot, value)
                forward(it + 1, slot, slot == 0)

            collect(near_a, own_a.at[it], share_relay, share_recv, renew)
            state = out_ref

    spread(mine.at[:, cols(off)], near, fetch_send, fetch_recv, finish)
    relay(near, fetch_relay, fetch_recv, finish)
    spread(part_a.at[0], near_a, share_send, share_recv, finish)
    relay(near_a, share_relay, share_recv, finish)
    for it in range(ITERS):
        for slot in range(slots):
            for q in range(n_off):
                def gone():
                    copy(back.at[it, slot, q], ret.at[it, off, slot], ret_send.at[it, slot, q],
                         ret_recv.at[it, off, slot], row_at(1), q).wait_send()

                if slot:
                    gone()
                else:
                    pl.when(off != 0)(gone)
        for step in range(1, n_off):
            copy(direct.at[it, 0], ret.at[it, off, slots], ret_send.at[it, slots, step],
                 ret_recv.at[it, off, slots], me, peer(step)).wait_send()
            copy(part_a.at[it], part_a.at[it], peer_send.at[it, step],
                 peer_recv.at[it, off], me, peer(step)).wait_send()

        def dealt(step, carry):
            index = lax.rem(me * owners + lax.rem(off, owners) + step, n * owners)
            copy(gram_sum.at[it], gram_sum.at[it], gs_send.at[it, index],
                 gs_recv.at[it, 0], row_at(1), off).wait_send()
            return carry

        def told(step, carry):
            target = lax.rem(flat_me + step, devices)
            copy(gram_sum.at[it], gram_sum.at[it], ga_send.at[it, target],
                 ga_recv.at[it, 0], row_at(1), off).wait_send()
            return carry

        lax.fori_loop(1, n * owners, dealt, 0, unroll=small)
        if owners == n_off:
            lax.fori_loop(1, devices, told, 0, unroll=small)
        else:
            @pl.when(off < owners)
            def _():
                lax.fori_loop(1, devices, told, 0)

            @pl.when(off >= owners)
            def _():
                dealt(0, 0)


def local(n, n_off, vectors, tiles, live, energies, precond):
    k, width = vectors.shape
    slots = tiles.shape[1] // width
    part = width // n_off
    owners = min(n_off, 2 * k // n)
    grow = 2 * k // (n * owners)
    outside = pl.BlockSpec(memory_space=pl.ANY)
    f32, b16 = jnp.float32, jnp.bfloat16
    vmem, dma = pltpu.VMEM, pltpu.SemaphoreType.DMA
    inside = pl.BlockSpec(memory_space=pltpu.VMEM)
    return pl.pallas_call(
        functools.partial(kernel, n, n_off, slots, float(width * n)),
        out_shape=(
            jax.ShapeDtypeStruct((k, width), f32),
            jax.ShapeDtypeStruct((k, k), f32),
        ),
        in_specs=[outside] * 5,
        out_specs=(inside, inside),
        scratch_shapes=[
            vmem((k, width), f32),
            pltpu.SMEM((1, slots), jnp.int32),
            vmem((1, width), f32),
            vmem((1, width), f32),
            vmem((k, part), f32),
            vmem((ITERS, slots, n_off, k, part), f32),
            vmem((slots, width, width), f32),
            vmem((slots, width, width), b16),
            vmem((slots, width, width), b16),
            vmem((k + 8, width), f32),
            vmem((slots, k + 8, width), f32),
            vmem((slots + 1, 2 * k, width), b16),
            vmem((ITERS, n_off, k, part), f32),
            vmem((ITERS, slots, n_off, k, part), f32),
            vmem((ITERS, n_off, slots + 1, k, part), f32),
            vmem((ITERS, k, part), f32),
            vmem((ITERS, k, width), f32),
            vmem((slots, k, width), f32),
            vmem((ITERS, n * owners, grow, 2 * k), f32),
            vmem((ITERS, n * n_off, grow, 2 * k), f32),
            vmem((ITERS, grow, 2 * k), f32),
            vmem((ITERS, n * owners, grow, 2 * k), f32),
            dma((slots + 4,)),
            dma((ITERS, slots, n_off)),
            dma((slots, n_off)),
            dma((slots, n_off)),
            dma((n_off * slots,)),
            dma((slots, n_off)),
            dma((ITERS, slots + 1, n_off)),
            dma((ITERS, n_off, slots + 1)),
            dma((n_off * slots,)),
            dma((slots, n_off)),
            dma((ITERS, n_off)),
            dma((ITERS, n_off)),
            dma((ITERS, n * owners)),
            dma((ITERS, n * n_off)),
            dma((ITERS, n * n_off)),
            dma((ITERS, n * owners)),
        ],
        compiler_params=pltpu.CompilerParams(
            collective_id=0, has_side_effects=True, vmem_limit_bytes=60 * 1024 * 1024
        ),
    )(vectors, tiles, live, energies[None, :], precond[None, :])


def solution(mesh):
    placed = (P(None, "row"), P("row", "off"), P("row", "off"), P("row"), P("row"))
    return jax.shard_map(
        functools.partial(local, mesh.shape["row"], mesh.shape["off"]),
        mesh=mesh, in_specs=placed, out_specs=(P(None, "row"), P()), check_vma=False,
    )
```

time: 82.7 us -> 71.5 us (0.86)
  Pallas kernels: 77.6 us -> 67.6 us
  local copies, waits for them, and re-layouts: 4.29 us -> 3.05 us
    pallas_call x1, Pallas kernels: 77.6 us -> 67.6 us  [local(): pl.pallas_call(functools.partial(kernel, n, n_off, slots, float(width * n...]
    unnamed x10 -> x2, local copies, waits for them, and re-layouts: 4.29 us -> 3.05 us
where the time goes in v2:
time: 71.5 us; the launch traced here: 71.3 us
  Pallas kernels  67.6 us (95%)
  local copies, waits for them, and re-layouts  3.05 us (4%)
    pallas_call x1, Pallas kernels, local(): pl.pallas_call(functools.partial(kernel, n, n_off, slots, float(width * n...  67.6 us
    unnamed x2, local copies, waits for them, and re-layouts  3.05 us

profile of v2, /device:TPU:0, one launch (start us, length us, event | category | flops | bytes accessed | tf_op | source)
XLA Modules:
  0.0 71.3 jit_solution(5415914708052034412)
XLA Ops:
  0.6 67.6 %shard_map.68 = (f32[64,1024]{1,0:T(8,128)}, f32[64,64]{1,0:T(8,128)}) custom-call(f32[64,1024]{1,0:T(8,128)} %vec_hbm.1, f32[1024,2048]{1,0:T(8,128)} %tiles_ref.1, s32[1,2]{1,0:T(1,128)} %live_hbm.1, f32[1,1024]{1,0:T(1,128)} %bitcast.2, f32[1,1024]{1,0:T(1,128)} %bitcast.3), custom_call_target="tpu_custom_call" | custom-call | tf_op jit(solution)/shard_map/pallas_call | solution.py:452
  68.2 1.7 %copy.9 = f32[64,1024]{1,0:T(8,128)} copy(f32[64,1024]{1,0:T(8,128)} %get-tuple-element.4) | data formatting | bytes 524288
  69.9 1.4 %copy.10 = f32[64,64]{1,0:T(8,128)} copy(f32[64,64]{1,0:T(8,128)} %get-tuple-element.5) | data formatting | bytes 32768

commit v3 on v2

--- a/solution.py
+++ b/solution.py
@@ -8,6 +8,8 @@
 from jax.sharding import PartitionSpec as P
 
 ITERS = 2
+APPS = 3
+GRANT = 60 * 1024 * 1024
 MESH = pl.DeviceIdType.MESH
 NN = (((1,), (0,)), ((), ()))
 NT = (((1,), (1,)), ((), ()))
@@ -152,42 +154,41 @@
 
     put_split(slots, vec_ref[...])
 
-    def transposed(it, slot):
-        shift = off * slots + slot
+    def transposed(app, slot):
         for q in range(n_off):
             for c in range(part // chunk):
                 at = pl.ds(q * part + c * chunk, chunk)
                 both = coarse(split[slots], high[slot, :, at], NN)
                 rest = coarse(split[slots, :k, :], low[slot, :, at], NN)
-                back[it, slot, q, :, pl.ds(c * chunk, chunk)] = both[:k] + both[k:] + rest
-
+                back[app, slot, q, :, pl.ds(c * chunk, chunk)] = both[:k] + both[k:] + rest
+            if slot:
+                @pl.when(jnp.logical_not(odd))
+                def _():
+                    copy(
+                        back.at[app, slot, q], hand.at[app, slot - 1, q],
+                        ret_send.at[app, slot, q], hand_recv.at[app, slot - 1, q],
+                        row_at(1), off,
+                    ).start()
+
+    def deliver(app, slot):
+        shift = off * slots + slot
+        for q in range(n_off):
             if slot < slots - 1:
                 @pl.when(odd)
                 def _():
-                    where = hand.at[it, slot, q]
-                    copy(where, where, hand_recv.at[it, slot, q], hand_recv.at[it, slot, q],
-                         row_at(1), off).wait_recv()
-                    back[it, slot, q] = back[it, slot, q] + hand[it, slot, q]
+                    where = hand.at[app, slot, q]
+                    copy(where, where, hand_recv.at[app, slot, q],
+                         hand_recv.at[app, slot, q], row_at(1), off).wait_recv()
+                    back[app, slot, q] = back[app, slot, q] + hand[app, slot, q]
 
             def away():
                 copy(
-                    back.at[it, slot, q], ret.at[it, off, slot],
-                    ret_send.at[it, slot, q], ret_recv.at[it, off, slot],
+                    back.at[app, slot, q], ret.at[app, off, slot],
+                    ret_send.at[app, slot, q], ret_recv.at[app, off, slot],
                     row_at(shift), q,
                 ).start()
 
-            if slot:
-                pl.when(odd)(away)
-
-                @pl.when(jnp.logical_not(odd))
-                def _():
-                    copy(
-                        back.at[it, slot, q], hand.at[it, slot - 1, q],
-                        ret_send.at[it, slot, q], hand_recv.at[it, slot - 1, q],
-                        row_at(1), off,
-                    ).start()
-            else:
-                pl.when(shift != 0)(away)
+            pl.when(odd if slot else shift != 0)(away)
 
     def forward(it, slot, first):
         for c in range(width // chunk):
@@ -218,6 +219,7 @@
 
         lax.fori_loop(0, width // rows, cut, 0)
         transposed(0, slot)
+        deliver(0, slot)
 
     def collect(dst, own, send, recv, use):
         for slot in range(slots):
@@ -241,38 +243,28 @@
             == lax.broadcasted_iota(jnp.int32, (k, k), 1)
         ).astype(jnp.float32)
 
-    state = mine
-    for it in range(ITERS):
-        last = it == ITERS - 1
-        if it == 0:
-            def use(slot):
-                put_split(slot, near[slot, :k, :])
-                forward(0, slot, slot == 0)
-
-            collect(near, mine, fetch_relay, fetch_recv, use)
-
+    def exchange(app):
         @pl.when(off == 0)
         def _():
             for q in range(n_off):
-                direct[it, q] = direct[it, q] + back[it, 0, q]
+                direct[app, q] = direct[app, q] + back[app, 0, q]
 
         for step in range(1, n_off):
             copy(
-                direct.at[it, peer(step)], ret.at[it, off, slots],
-                ret_send.at[it, slots, step], ret_recv.at[it, off, slots],
+                direct.at[app, peer(step)], ret.at[app, off, slots],
+                ret_send.at[app, slots, step], ret_recv.at[app, off, slots],
                 me, peer(step),
             ).start()
 
-        x_part = state[:k, cols(off)]
-        p_part = precond_ref[:, cols(off)]
-        acc[...] = energy_ref[:, cols(off)] * x_part + direct[it, off]
+    def image(app, value):
+        acc[...] = energy_ref[:, cols(off)] * value + direct[app, off]
         for group in range(n_off):
             for slot in range(slots):
                 def take():
-                    where = ret.at[it, group, slot]
-                    copy(where, where, ret_send.at[it, 0, 0], ret_recv.at[it, group, slot],
+                    where = ret.at[app, group, slot]
+                    copy(where, where, ret_send.at[app, 0, 0], ret_recv.at[app, group, slot],
                          row_at(1), off).wait_recv()
-                    acc[...] = acc[...] + ret[it, group, slot]
+                    acc[...] = acc[...] + ret[app, group, slot]
 
                 if slot:
                     pl.when(lax.rem(me + group * slots + slot, 2) == 1)(take)
@@ -280,11 +272,39 @@
                     take()
         total = acc[...]
         for step in range(1, n_off):
-            where = ret.at[it, peer(step), slots]
-            copy(where, where, ret_send.at[it, 0, 0], ret_recv.at[it, peer(step), slots],
+            where = ret.at[app, peer(step), slots]
+            copy(where, where, ret_send.at[app, 0, 0], ret_recv.at[app, peer(step), slots],
                  row_at(1), off).wait_recv()
-            total = total + ret[it, peer(step), slots]
-
+            total = total + ret[app, peer(step), slots]
+        return total
+
+    def use_first(slot):
+        put_split(slot, near[slot, :k, :])
+        forward(0, slot, slot == 0)
+
+    collect(near, mine, fetch_relay, fetch_recv, use_first)
+    exchange(0)
+
+    put_split(slots, precond_ref[...] * vec_ref[...])
+    for slot in order:
+        transposed(1, slot)
+    for slot in range(slots):
+        put_split(slot, near[slot, k : k + 1, :] * near[slot, :k, :])
+        forward(1, slot, slot == 0)
+
+    p_part = precond_ref[:, cols(off)]
+
+    for it in range(ITERS):
+        last = it == ITERS - 1
+        if it == 0:
+            x_part = vec_ref[:, cols(off)]
+            total = image(0, x_part)
+        else:
+            x_part = out_ref[:, cols(off)]
+            b_part = p_part * vec_ref[:, cols(off)]
+            total_b = image(1, b_part)
+            total_a = image(2, part_a[0])
+            total = triple(both_fix, jnp.concatenate([total_a, total_b], axis=0))
         a_part = x_part - p_part * total
         part_a[it] = a_part
         own_a[it, :, cols(off)] = a_part
@@ -295,6 +315,9 @@
             ).start()
         if not last:
             spread(part_a.at[it], near_a, share_send, share_recv, begin)
+            for slot in order:
+                deliver(1, slot)
+            exchange(1)
 
         ab = jnp.concatenate([a_part, p_part * x_part], axis=0)
         inner = triple(ab, ab, NT)
@@ -347,6 +370,15 @@
             lax.fori_loop(1, devices, tell, 0, unroll=small)
 
         lax.fori_loop(1, n * owners, deal, 0, unroll=small)
+        for step in range(1, n_off):
+            where = own_a.at[it, :, cols(peer(step))]
+            copy(where, where, peer_send.at[it, step], peer_recv.at[it, peer(step)],
+                 row_at(1), off).wait_recv()
+        if not last:
+            put_split(slots, own_a[0])
+            for slot in order:
+                transposed(2, slot)
+                deliver(2, slot)
         if owners == n_off:
             own()
         else:
@@ -357,6 +389,13 @@
                 deal(0, 0)
                 hear(0, 0)
 
+        if not last:
+            def use_second(slot):
+                put_split(slot, near_a[slot])
+                forward(2, slot, slot == 0)
+
+            collect(near_a, own_a.at[0], share_relay, share_recv, use_second)
+            exchange(2)
         lax.fori_loop(1, n * owners, hear, 0, unroll=small)
         full = gram_all[it].reshape(2 * k, 2 * k) / total_rows
         turned = full.T
@@ -367,50 +406,35 @@
         fix = 1.5 * eye() - 0.5 * overlap
         both_fix = jnp.concatenate([fix, triple(fix, ritz_t)], axis=1)
 
-        def update(a_value, x_value, p_row):
-            return triple(both_fix, jnp.concatenate([a_value, p_row * x_value], axis=0))
-
-        for step in range(1, n_off):
-            where = own_a.at[it, :, cols(peer(step))]
-            copy(where, where, peer_send.at[it, step], peer_recv.at[it, peer(step)],
-                 row_at(1), off).wait_recv()
-        fresh = update(own_a[it], state[:k, :], precond_ref[...])
-        out_ref[...] = fresh
+        state = vec_ref if it == 0 else out_ref
+        out_ref[...] = triple(
+            both_fix,
+            jnp.concatenate([own_a[it], precond_ref[...] * state[...]], axis=0),
+        )
         if last:
             ritz_ref[...] = ritz
-        else:
-            put_split(slots, fresh)
-            for slot in order:
-                transposed(it + 1, slot)
-
-            def renew(slot):
-                value = update(
-                    near_a[slot], near[slot, :k, :], near[slot, k : k + 1, :]
-                )
-                put_split(slot, value)
-                forward(it + 1, slot, slot == 0)
-
-            collect(near_a, own_a.at[it], share_relay, share_recv, renew)
-            state = out_ref
 
     spread(mine.at[:, cols(off)], near, fetch_send, fetch_recv, finish)
     relay(near, fetch_relay, fetch_recv, finish)
     spread(part_a.at[0], near_a, share_send, share_recv, finish)
     relay(near_a, share_relay, share_recv, finish)
-    for it in range(ITERS):
+    for app in range(APPS):
         for slot in range(slots):
             for q in range(n_off):
                 def gone():
-                    copy(back.at[it, slot, q], ret.at[it, off, slot], ret_send.at[it, slot, q],
-                         ret_recv.at[it, off, slot], row_at(1), q).wait_send()
+                    copy(back.at[app, slot, q], ret.at[app, off, slot],
+                         ret_send.at[app, slot, q], ret_recv.at[app, off, slot],
+                         row_at(1), q).wait_send()
 
                 if slot:
                     gone()
                 else:
                     pl.when(off != 0)(gone)
         for step in range(1, n_off):
-            copy(direct.at[it, 0], ret.at[it, off, slots], ret_send.at[it, slots, step],
-                 ret_recv.at[it, off, slots], me, peer(step)).wait_send()
+            copy(direct.at[app, 0], ret.at[app, off, slots], ret_send.at[app, slots, step],
+                 ret_recv.at[app, off, slots], me, peer(step)).wait_send()
+    for it in range(ITERS):
+        for step in range(1, n_off):
             copy(part_a.at[it], part_a.at[it], peer_send.at[it, step],
                  peer_recv.at[it, off], me, peer(step)).wait_send()
 
@@ -437,6 +461,17 @@
             @pl.when(off >= owners)
             def _():
                 dealt(0, 0)
+
+
+def hand_over(basis_in, ritz_in, basis_out, ritz_out, sems):
+    moves = [
+        pltpu.make_async_copy(basis_in, basis_out, sems.at[0]),
+        pltpu.make_async_copy(ritz_in, ritz_out, sems.at[1]),
+    ]
+    for one in moves:
+        one.start()
+    for one in moves:
+        one.wait()
 
 
 def local(n, n_off, vectors, tiles, live, energies, precond):
@@ -449,7 +484,7 @@
     f32, b16 = jnp.float32, jnp.bfloat16
     vmem, dma = pltpu.VMEM, pltpu.SemaphoreType.DMA
     inside = pl.BlockSpec(memory_space=pltpu.VMEM)
-    return pl.pallas_call(
+    basis, ritz = pl.pallas_call(
         functools.partial(kernel, n, n_off, slots, float(width * n)),
         out_shape=(
             jax.ShapeDtypeStruct((k, width), f32),
@@ -463,16 +498,16 @@
             vmem((1, width), f32),
             vmem((1, width), f32),
             vmem((k, part), f32),
-            vmem((ITERS, slots, n_off, k, part), f32),
+            vmem((APPS, slots, n_off, k, part), f32),
             vmem((slots, width, width), f32),
             vmem((slots, width, width), b16),
             vmem((slots, width, width), b16),
             vmem((k + 8, width), f32),
             vmem((slots, k + 8, width), f32),
             vmem((slots + 1, 2 * k, width), b16),
-            vmem((ITERS, n_off, k, part), f32),
-            vmem((ITERS, slots, n_off, k, part), f32),
-            vmem((ITERS, n_off, slots + 1, k, part), f32),
+            vmem((APPS, n_off, k, part), f32),
+            vmem((APPS, slots, n_off, k, part), f32),
+            vmem((APPS, n_off, slots + 1, k, part), f32),
             vmem((ITERS, k, part), f32),
             vmem((ITERS, k, width), f32),
             vmem((slots, k, width), f32),
@@ -481,13 +516,13 @@
             vmem((ITERS, grow, 2 * k), f32),
             vmem((ITERS, n * owners, grow, 2 * k), f32),
             dma((slots + 4,)),
-            dma((ITERS, slots, n_off)),
+            dma((APPS, slots, n_off)),
             dma((slots, n_off)),
             dma((slots, n_off)),
             dma((n_off * slots,)),
             dma((slots, n_off)),
-            dma((ITERS, slots + 1, n_off)),
-            dma((ITERS, n_off, slots + 1)),
+            dma((APPS, slots + 1, n_off)),
+            dma((APPS, n_off, slots + 1)),
             dma((n_off * slots,)),
             dma((slots, n_off)),
             dma((ITERS, n_off)),
@@ -498,9 +533,20 @@
             dma((ITERS, n * owners)),
         ],
         compiler_params=pltpu.CompilerParams(
-            collective_id=0, has_side_effects=True, vmem_limit_bytes=60 * 1024 * 1024
+            collective_id=0, has_side_effects=True, vmem_limit_bytes=GRANT
         ),
     )(vectors, tiles, live, energies[None, :], precond[None, :])
+    return pl.pallas_call(
+        hand_over,
+        out_shape=(
+            jax.ShapeDtypeStruct((k, width), f32),
+            jax.ShapeDtypeStruct((k, k), f32),
+        ),
+        in_specs=[outside] * 2,
+        out_specs=(outside, outside),
+        scratch_shapes=[dma((2,))],
+        compiler_params=pltpu.CompilerParams(vmem_limit_bytes=GRANT),
+    )(basis, ritz)
 
 
 def solution(mesh):

time: 71.5 us -> 75.6 us (1.057)
  Pallas kernels: 67.6 us -> 74.8 us
  local copies, waits for them, and re-layouts: 3.05 us -> 0 us
    pallas_call x0 -> x1, Pallas kernels: none -> 10.1 us  [local(): pl.pallas_call(hand_over, out_shape=(jax.ShapeDtypeStruct((k, width), f32...]
    unnamed x2 -> x0, local copies, waits for them, and re-layouts: 3.05 us -> none
    pallas_call x1, Pallas kernels: 67.6 us -> 64.7 us  [local(): pl.pallas_call(functools.partial(kernel, n, n_off, slots, float(width * n...]
where the time goes in v3:
time: 75.6 us; the launch traced here: 75.4 us
  Pallas kernels  74.8 us (99%)
    pallas_call x1, Pallas kernels, local(): pl.pallas_call(functools.partial(kernel, n, n_off, slots, float(width * n...  64.7 us
    pallas_call x1, Pallas kernels, local(): pl.pallas_call(hand_over, out_shape=(jax.ShapeDtypeStruct((k, width), f32...  10.1 us

profile of v3, /device:TPU:0, one launch (start us, length us, event | category | flops | bytes accessed | tf_op | source)
XLA Modules:
  0.0 75.4 jit_solution(113749644458287517)
XLA Ops:
  0.6 64.7 %shard_map.68 = (f32[64,1024]{1,0:T(8,128)}, f32[64,64]{1,0:T(8,128)}) custom-call(f32[64,1024]{1,0:T(8,128)} %vec_hbm.1, f32[1024,2048]{1,0:T(8,128)} %tiles_ref.1, s32[1,2]{1,0:T(1,128)} %live_hbm.1, f32[1,1024]{1,0:T(1,128)} %bitcast.2, f32[1,1024]{1,0:T(1,128)} %bitcast.3), custom_call_target="tpu_custom_call" | custom-call | tf_op jit(solution)/shard_map/pallas_call | solution.py:487
  65.4 10.1 %shard_map.69 = (f32[64,1024]{1,0:T(8,128)}, f32[64,64]{1,0:T(8,128)}) custom-call(f32[64,1024]{1,0:T(8,128)} %get-tuple-element.4.basis_in, f32[64,64]{1,0:T(8,128)} %get-tuple-element.5.ritz_in), custom_call_target="tpu_custom_call" | custom-call | tf_op jit(solution)/shard_map/pallas_call | solution.py:539

commit v4 on v3

--- a/solution.py
+++ b/solution.py
@@ -33,23 +33,32 @@
     return both[:count] + both[count:] + coarse(left_hi, right_lo, dims)
 
 
+def shares(n, n_off, k):
+    block = 4 if n % 4 == 0 else 1
+    while 2 * k % (block * n_off):
+        block //= 2
+    team = block * n_off
+    return block, team, n // block, 2 * k // team
+
+
 def kernel(
     n, n_off, slots, total_rows,
     vec_hbm, tiles_ref, live_hbm, energy_hbm, precond_hbm,
     out_ref, ritz_ref,
     vec_ref, live_ref, energy_ref, precond_ref, acc, hand,
     raw, high, low, mine, near, split, direct, back, ret, part_a, own_a, near_a,
-    gram, gram_in, gram_sum, gram_all,
+    gram, gram_in, gram_off, gram_sum, gram_all,
     load_sem, hand_recv, fetch_relay, share_relay, fetch_send, fetch_recv, ret_send, ret_recv, share_send, share_recv,
-    peer_send, peer_recv, gs_send, gs_recv, ga_send, ga_recv,
+    peer_send, peer_recv, gs_send, gs_recv, go_send, go_recv, ga_send, ga_recv,
 ):
     me = lax.axis_index("row")
     off = lax.axis_index("off")
     k, width = vec_ref.shape
     part = width // n_off
     chunk = min(256, part)
-    owners = min(n_off, 2 * k // n)
-    grow = 2 * k // (n * owners)
+    block, team, floors, grow = shares(n, n_off, k)
+    floor, base = me // block, me - lax.rem(me, block)
+    spot = lax.rem(me, block) * n_off + off
     devices = n * n_off
     flat_me = me * n_off + off
     odd = lax.rem(me, 2) == 1
@@ -148,27 +157,40 @@
     spread(mine.at[:, cols(off)], near, fetch_send, fetch_recv, begin)
 
     def put_split(where, value):
+        count = value.shape[0]
         hi, lo = halves(value)
-        split[where, :k, :] = hi
-        split[where, k:, :] = lo
-
-    put_split(slots, vec_ref[...])
-
-    def transposed(app, slot):
+        split[where, :count, :] = hi
+        split[where, count : 2 * count, :] = lo
+
+    def pair(value, p_row):
+        return jnp.concatenate([value, p_row * value], axis=0)
+
+    put_split(slots, pair(vec_ref[...], precond_ref[...]))
+
+    def transposed(apps, slot):
+        count = k * len(apps)
         for q in range(n_off):
             for c in range(part // chunk):
                 at = pl.ds(q * part + c * chunk, chunk)
-                both = coarse(split[slots], high[slot, :, at], NN)
-                rest = coarse(split[slots, :k, :], low[slot, :, at], NN)
-                back[app, slot, q, :, pl.ds(c * chunk, chunk)] = both[:k] + both[k:] + rest
-            if slot:
-                @pl.when(jnp.logical_not(odd))
-                def _():
-                    copy(
-                        back.at[app, slot, q], hand.at[app, slot - 1, q],
-                        ret_send.at[app, slot, q], hand_recv.at[app, slot - 1, q],
-                        row_at(1), off,
-                    ).start()
+                both = coarse(split[slots, : 2 * count, :], high[slot, :, at], NN)
+                rest = coarse(split[slots, :count, :], low[slot, :, at], NN)
+                term = both[:count] + both[count:] + rest
+                for index, app in enumerate(apps):
+                    back[app, slot, q, :, pl.ds(c * chunk, chunk)] = (
+                        term[index * k : (index + 1) * k]
+                    )
+            for app in apps:
+                hand_on(app, slot, q)
+
+    def hand_on(app, slot, q):
+        if slot:
+            @pl.when(jnp.logical_not(odd))
+            def _():
+                copy(
+                    back.at[app, slot, q], hand.at[app, slot - 1, q],
+                    ret_send.at[app, slot, q], hand_recv.at[app, slot - 1, q],
+                    row_at(1), off,
+                ).start()
 
     def deliver(app, slot):
         shift = off * slots + slot
@@ -190,18 +212,21 @@
 
             pl.when(odd if slot else shift != 0)(away)
 
-    def forward(it, slot, first):
+    def forward(apps, slot, first):
+        count = k * len(apps)
         for c in range(width // chunk):
             at = pl.ds(c * chunk, chunk)
-            both = coarse(split[slot], high[slot, at, :], NT)
-            rest = coarse(split[slot, :k, :], low[slot, at, :], NT)
-            term = both[:k] + both[k:] + rest
+            both = coarse(split[slot, : 2 * count, :], high[slot, at, :], NT)
+            rest = coarse(split[slot, :count, :], low[slot, at, :], NT)
+            term = both[:count] + both[count:] + rest
             q, place = (c * chunk) // part, (c * chunk) % part
             where = pl.ds(place, chunk)
-            if first:
-                direct[it, q, :, where] = term
-            else:
-                direct[it, q, :, where] = direct[it, q, :, where] + term
+            for index, app in enumerate(apps):
+                one = term[index * k : (index + 1) * k]
+                if first:
+                    direct[app, q, :, where] = one
+                else:
+                    direct[app, q, :, where] = direct[app, q, :, where] + one
 
     rows = 32
     for slot in order:
@@ -218,7 +243,7 @@
             return carry
 
         lax.fori_loop(0, width // rows, cut, 0)
-        transposed(0, slot)
+        transposed((0, 1), slot)
         deliver(0, slot)
 
     def collect(dst, own, send, recv, use):
@@ -279,18 +304,11 @@
         return total
 
     def use_first(slot):
-        put_split(slot, near[slot, :k, :])
-        forward(0, slot, slot == 0)
+        put_split(slot, pair(near[slot, :k, :], near[slot, k : k + 1, :]))
+        forward((0, 1), slot, slot == 0)
 
     collect(near, mine, fetch_relay, fetch_recv, use_first)
     exchange(0)
-
-    put_split(slots, precond_ref[...] * vec_ref[...])
-    for slot in order:
-        transposed(1, slot)
-    for slot in range(slots):
-        put_split(slot, near[slot, k : k + 1, :] * near[slot, :k, :])
-        forward(1, slot, slot == 0)
 
     p_part = precond_ref[:, cols(off)]
 
@@ -324,52 +342,19 @@
         xy = triple(x_part, total, NT)
         low_half = jnp.concatenate([xy, inner[k:, k:]], axis=1)
         packed = jnp.concatenate([inner[:k, :], low_half], axis=0)
-        for t in range(n * owners):
+        for t in range(team):
             gram[it, t] = packed[t * grow : (t + 1) * grow, :]
 
-        def owner_at(step):
-            index = lax.rem(me * owners + lax.rem(off, owners) + step, n * owners)
-            return index, index // owners, lax.rem(index, owners)
-
-        def deal(step, carry):
-            index, row, col = owner_at(step)
+        def mate(step):
+            index = lax.rem(spot + step, team)
+            return index, base + index // n_off, lax.rem(index, n_off)
+
+        for step in range(1, team):
+            index, row, col = mate(step)
             copy(
-                gram.at[it, index], gram_in.at[it, flat_me], gs_send.at[it, index],
-                gs_recv.at[it, flat_me], row, col,
+                gram.at[it, index], gram_in.at[it, spot], gs_send.at[it, step],
+                gs_recv.at[it, spot], row, col,
             ).start()
-            return carry
-
-        def add(step, piece):
-            source = lax.rem(flat_me + step, devices)
-            where = gram_in.at[it, source]
-            copy(where, where, gs_send.at[it, 0], gs_recv.at[it, source],
-                 row_at(1), off).wait_recv()
-            return piece + gram_in[it, source]
-
-        def tell(step, carry):
-            target = lax.rem(flat_me + step, devices)
-            copy(
-                gram_sum.at[it], gram_all.at[it, me * owners + off], ga_send.at[it, target],
-                ga_recv.at[it, me * owners + off], target // n_off, lax.rem(target, n_off),
-            ).start()
-            return carry
-
-        def hear(step, carry):
-            index = owner_at(step)[0]
-            where = gram_all.at[it, index]
-            copy(where, where, ga_send.at[it, 0], ga_recv.at[it, index],
-                 row_at(1), off).wait_recv()
-            return carry
-
-        def own():
-            piece = lax.fori_loop(
-                1, devices, add, gram[it, me * owners + off], unroll=small
-            )
-            gram_sum[it] = piece
-            gram_all[it, me * owners + off] = piece
-            lax.fori_loop(1, devices, tell, 0, unroll=small)
-
-        lax.fori_loop(1, n * owners, deal, 0, unroll=small)
         for step in range(1, n_off):
             where = own_a.at[it, :, cols(peer(step))]
             copy(where, where, peer_send.at[it, step], peer_recv.at[it, peer(step)],
@@ -377,26 +362,50 @@
         if not last:
             put_split(slots, own_a[0])
             for slot in order:
-                transposed(2, slot)
+                transposed((2,), slot)
                 deliver(2, slot)
-        if owners == n_off:
-            own()
-        else:
-            pl.when(off < owners)(own)
-
-            @pl.when(off >= owners)
-            def _():
-                deal(0, 0)
-                hear(0, 0)
-
+        piece = gram[it, spot]
+        for step in range(1, team):
+            index = mate(step)[0]
+            where = gram_in.at[it, index]
+            copy(where, where, gs_send.at[it, step], gs_recv.at[it, index],
+                 row_at(1), off).wait_recv()
+            piece = piece + gram_in[it, index]
+        gram_off[it, floor] = piece
+        for step in range(1, floors):
+            copy(
+                gram_off.at[it, floor], gram_off.at[it, floor], go_send.at[it, step],
+                go_recv.at[it, floor], row_at(step * block), off,
+            ).start()
+
+        for step in range(1, floors):
+            index = lax.rem(floor + step, floors)
+            where = gram_off.at[it, index]
+            copy(where, where, go_send.at[it, step], go_recv.at[it, index],
+                 row_at(1), off).wait_recv()
+        piece = gram_off[it, 0]
+        for index in range(1, floors):
+            piece = piece + gram_off[it, index]
+        gram_sum[it] = piece
+        gram_all[it, spot] = piece
+        for step in range(1, team):
+            index, row, col = mate(step)
+            copy(
+                gram_sum.at[it], gram_all.at[it, spot], ga_send.at[it, step],
+                ga_recv.at[it, spot], row, col,
+            ).start()
         if not last:
             def use_second(slot):
                 put_split(slot, near_a[slot])
-                forward(2, slot, slot == 0)
+                forward((2,), slot, slot == 0)
 
             collect(near_a, own_a.at[0], share_relay, share_recv, use_second)
             exchange(2)
-        lax.fori_loop(1, n * owners, hear, 0, unroll=small)
+        for step in range(1, team):
+            index = mate(step)[0]
+            where = gram_all.at[it, index]
+            copy(where, where, ga_send.at[it, step], ga_recv.at[it, index],
+                 row_at(1), off).wait_recv()
         full = gram_all[it].reshape(2 * k, 2 * k) / total_rows
         turned = full.T
         ritz, ritz_t = full[k:, :k], turned[:k, k:]
@@ -438,29 +447,14 @@
             copy(part_a.at[it], part_a.at[it], peer_send.at[it, step],
                  peer_recv.at[it, off], me, peer(step)).wait_send()
 
-        def dealt(step, carry):
-            index = lax.rem(me * owners + lax.rem(off, owners) + step, n * owners)
-            copy(gram_sum.at[it], gram_sum.at[it], gs_send.at[it, index],
+        for step in range(1, team):
+            copy(gram_sum.at[it], gram_sum.at[it], gs_send.at[it, step],
                  gs_recv.at[it, 0], row_at(1), off).wait_send()
-            return carry
-
-        def told(step, carry):
-            target = lax.rem(flat_me + step, devices)
-            copy(gram_sum.at[it], gram_sum.at[it], ga_send.at[it, target],
+            copy(gram_sum.at[it], gram_sum.at[it], ga_send.at[it, step],
                  ga_recv.at[it, 0], row_at(1), off).wait_send()
-            return carry
-
-        lax.fori_loop(1, n * owners, dealt, 0, unroll=small)
-        if owners == n_off:
-            lax.fori_loop(1, devices, told, 0, unroll=small)
-        else:
-            @pl.when(off < owners)
-            def _():
-                lax.fori_loop(1, devices, told, 0)
-
-            @pl.when(off >= owners)
-            def _():
-                dealt(0, 0)
+        for step in range(1, floors):
+            copy(gram_sum.at[it], gram_sum.at[it], go_send.at[it, step],
+                 go_recv.at[it, 0], row_at(1), off).wait_send()
 
 
 def hand_over(basis_in, ritz_in, basis_out, ritz_out, sems):
@@ -478,9 +472,8 @@
     k, width = vectors.shape
     slots = tiles.shape[1] // width
     part = width // n_off
-    owners = min(n_off, 2 * k // n)
-    grow = 2 * k // (n * owners)
-    outside = pl.BlockSpec(memory_space=pl.ANY)
+    _, team, floors, grow = shares(n, n_off, k)
+    outside = pl.BlockSpec(memory_space=pltpu.HBM)
     f32, b16 = jnp.float32, jnp.bfloat16
     vmem, dma = pltpu.VMEM, pltpu.SemaphoreType.DMA
     inside = pl.BlockSpec(memory_space=pltpu.VMEM)
@@ -504,17 +497,18 @@
             vmem((slots, width, width), b16),
             vmem((k + 8, width), f32),
             vmem((slots, k + 8, width), f32),
-            vmem((slots + 1, 2 * k, width), b16),
+            vmem((slots + 1, 4 * k, width), b16),
             vmem((APPS, n_off, k, part), f32),
             vmem((APPS, slots, n_off, k, part), f32),
             vmem((APPS, n_off, slots + 1, k, part), f32),
             vmem((ITERS, k, part), f32),
             vmem((ITERS, k, width), f32),
             vmem((slots, k, width), f32),
-            vmem((ITERS, n * owners, grow, 2 * k), f32),
-            vmem((ITERS, n * n_off, grow, 2 * k), f32),
+            vmem((ITERS, team, grow, 2 * k), f32),
+            vmem((ITERS, team, grow, 2 * k), f32),
+            vmem((ITERS, floors, grow, 2 * k), f32),
             vmem((ITERS, grow, 2 * k), f32),
-            vmem((ITERS, n * owners, grow, 2 * k), f32),
+            vmem((ITERS, team, grow, 2 * k), f32),
             dma((slots + 4,)),
             dma((APPS, slots, n_off)),
             dma((slots, n_off)),
@@ -527,10 +521,12 @@
             dma((slots, n_off)),
             dma((ITERS, n_off)),
             dma((ITERS, n_off)),
-            dma((ITERS, n * owners)),
-            dma((ITERS, n * n_off)),
-            dma((ITERS, n * n_off)),
-            dma((ITERS, n * owners)),
+            dma((ITERS, team)),
+            dma((ITERS, team)),
+            dma((ITERS, floors)),
+            dma((ITERS, floors)),
+            dma((ITERS, team)),
+            dma((ITERS, team)),
         ],
         compiler_params=pltpu.CompilerParams(
             collective_id=0, has_side_effects=True, vmem_limit_bytes=GRANT
@@ -542,7 +538,7 @@
             jax.ShapeDtypeStruct((k, width), f32),
             jax.ShapeDtypeStruct((k, k), f32),
         ),
-        in_specs=[outside] * 2,
+        in_specs=[inside] * 2,
         out_specs=(outside, outside),
         scratch_shapes=[dma((2,))],
         compiler_params=pltpu.CompilerParams(vmem_limit_bytes=GRANT),

time: 75.6 us -> 69.6 us (0.921)
  Pallas kernels: 74.8 us -> 68.8 us
    pallas_call x1, Pallas kernels: 10.1 us -> 1.67 us  [local(): pl.pallas_call(hand_over, out_shape=(jax.ShapeDtypeStruct((k, width), f32...]
    pallas_call x1, Pallas kernels: 64.7 us -> 67.2 us  [local(): pl.pallas_call(functools.partial(kernel, n, n_off, slots, float(width * n...]
where the time goes in v4:
time: 69.6 us; the launch traced here: 69.5 us
  Pallas kernels  68.8 us (99%)
    pallas_call x1, Pallas kernels, local(): pl.pallas_call(functools.partial(kernel, n, n_off, slots, float(width * n...  67.2 us
    pallas_call x1, Pallas kernels, local(): pl.pallas_call(hand_over, out_shape=(jax.ShapeDtypeStruct((k, width), f32...  1.67 us

profile of v4, /device:TPU:0, one launch (start us, length us, event | category | flops | bytes accessed | tf_op | source)
XLA Modules:
  0.0 69.5 jit_solution(16063134645884364662)
XLA Ops:
  0.6 67.2 %shard_map.68 = (f32[64,1024]{1,0:T(8,128)}, f32[64,64]{1,0:T(8,128)}) custom-call(f32[64,1024]{1,0:T(8,128)} %vec_hbm.1, f32[1024,2048]{1,0:T(8,128)} %tiles_ref.1, s32[1,2]{1,0:T(1,128)} %live_hbm.1, f32[1,1024]{1,0:T(1,128)} %bitcast.2, f32[1,1024]{1,0:T(1,128)} %bitcast.3), custom_call_target="tpu_custom_call" | custom-call | tf_op jit(solution)/shard_map/pallas_call | solution.py:480
  67.8 1.7 %shard_map.69 = (f32[64,1024]{1,0:T(8,128)}, f32[64,64]{1,0:T(8,128)}) custom-call(f32[64,1024]{1,0:T(8,128)} %get-tuple-element.4.basis_in, f32[64,64]{1,0:T(8,128)} %get-tuple-element.5.ritz_in), custom_call_target="tpu_custom_call" | custom-call | tf_op jit(solution)/shard_map/pallas_call | solution.py:535

commit v5 on v4

--- a/solution.py
+++ b/solution.py
@@ -9,6 +9,7 @@
 
 ITERS = 2
 APPS = 3
+SPAN = 128
 GRANT = 60 * 1024 * 1024
 MESH = pl.DeviceIdType.MESH
 NN = (((1,), (0,)), ((), ()))
@@ -48,7 +49,7 @@
     vec_ref, live_ref, energy_ref, precond_ref, acc, hand,
     raw, high, low, mine, near, split, direct, back, ret, part_a, own_a, near_a,
     gram, gram_in, gram_off, gram_sum, gram_all,
-    load_sem, hand_recv, fetch_relay, share_relay, fetch_send, fetch_recv, ret_send, ret_recv, share_send, share_recv,
+    load_sem, tile_sem, hand_recv, fetch_relay, share_relay, fetch_send, fetch_recv, ret_send, ret_recv, share_send, share_recv,
     peer_send, peer_recv, gs_send, gs_recv, go_send, go_recv, ga_send, ga_recv,
 ):
     me = lax.axis_index("row")
@@ -89,14 +90,20 @@
     for one in heads:
         one.start()
     order = list(range(slots - 1, -1, -1))
+    span = SPAN
     loads = [
-        pltpu.make_async_copy(
-            tiles_ref.at[:, pl.ds(slot * width, width)], raw.at[slot], load_sem.at[slot]
-        )
+        [
+            pltpu.make_async_copy(
+                tiles_ref.at[pl.ds(piece * span, span), pl.ds(slot * width, width)],
+                raw.at[slot, pl.ds(piece * span, span), :], tile_sem.at[slot, piece],
+            )
+            for piece in range(width // span)
+        ]
         for slot in range(slots)
     ]
     for slot in order:
-        loads[slot].start()
+        for one in loads[slot]:
+            one.start()
 
     barrier = pltpu.get_barrier_semaphore()
 
@@ -162,10 +169,7 @@
         split[where, :count, :] = hi
         split[where, count : 2 * count, :] = lo
 
-    def pair(value, p_row):
-        return jnp.concatenate([value, p_row * value], axis=0)
-
-    put_split(slots, pair(vec_ref[...], precond_ref[...]))
+    put_split(slots, vec_ref[...])
 
     def transposed(apps, slot):
         count = k * len(apps)
@@ -230,7 +234,6 @@
 
     rows = 32
     for slot in order:
-        loads[slot].wait()
         limit = live_ref[0, slot]
 
         def cut(index, carry):
@@ -242,8 +245,10 @@
             low[slot, pl.ds(start, rows), :] = lo
             return carry
 
-        lax.fori_loop(0, width // rows, cut, 0)
-        transposed((0, 1), slot)
+        for piece, one in enumerate(loads[slot]):
+            one.wait()
+            lax.fori_loop(piece * span // rows, (piece + 1) * span // rows, cut, 0)
+        transposed((0,), slot)
         deliver(0, slot)
 
     def collect(dst, own, send, recv, use):
@@ -304,11 +309,18 @@
         return total
 
     def use_first(slot):
-        put_split(slot, pair(near[slot, :k, :], near[slot, k : k + 1, :]))
-        forward((0, 1), slot, slot == 0)
+        put_split(slot, near[slot, :k, :])
+        forward((0,), slot, slot == 0)
 
     collect(near, mine, fetch_relay, fetch_recv, use_first)
     exchange(0)
+
+    put_split(slots, precond_ref[...] * vec_ref[...])
+    for slot in order:
+        transposed((1,), slot)
+    for slot in range(slots):
+        put_split(slot, near[slot, k : k + 1, :] * near[slot, :k, :])
+        forward((1,), slot, slot == 0)
 
     p_part = precond_ref[:, cols(off)]
 
@@ -319,8 +331,6 @@
             total = image(0, x_part)
         else:
             x_part = out_ref[:, cols(off)]
-            b_part = p_part * vec_ref[:, cols(off)]
-            total_b = image(1, b_part)
             total_a = image(2, part_a[0])
             total = triple(both_fix, jnp.concatenate([total_a, total_b], axis=0))
         a_part = x_part - p_part * total
@@ -378,6 +388,13 @@
                 go_recv.at[it, floor], row_at(step * block), off,
             ).start()
 
+        if not last:
+            def use_second(slot):
+                put_split(slot, near_a[slot])
+                forward((2,), slot, slot == 0)
+
+            collect(near_a, own_a.at[0], share_relay, share_recv, use_second)
+            exchange(2)
         for step in range(1, floors):
             index = lax.rem(floor + step, floors)
             where = gram_off.at[it, index]
@@ -395,12 +412,7 @@
                 ga_recv.at[it, spot], row, col,
             ).start()
         if not last:
-            def use_second(slot):
-                put_split(slot, near_a[slot])
-                forward((2,), slot, slot == 0)
-
-            collect(near_a, own_a.at[0], share_relay, share_recv, use_second)
-            exchange(2)
+            total_b = image(1, p_part * x_part)
         for step in range(1, team):
             index = mate(step)[0]
             where = gram_all.at[it, index]
@@ -497,7 +509,7 @@
             vmem((slots, width, width), b16),
             vmem((k + 8, width), f32),
             vmem((slots, k + 8, width), f32),
-            vmem((slots + 1, 4 * k, width), b16),
+            vmem((slots + 1, 2 * k, width), b16),
             vmem((APPS, n_off, k, part), f32),
             vmem((APPS, slots, n_off, k, part), f32),
             vmem((APPS, n_off, slots + 1, k, part), f32),
@@ -510,6 +522,7 @@
             vmem((ITERS, grow, 2 * k), f32),
             vmem((ITERS, team, grow, 2 * k), f32),
             dma((slots + 4,)),
+            dma((slots, width // SPAN)),
             dma((APPS, slots, n_off)),
             dma((slots, n_off)),
             dma((slots, n_off)),

time: 69.6 us -> 67.3 us (0.967)
  Pallas kernels: 68.8 us -> 66.6 us
    pallas_call x1, Pallas kernels: 67.2 us -> 64.9 us  [local(): pl.pallas_call(functools.partial(kernel, n, n_off, slots, float(width * n...]
where the time goes in v5:
time: 67.3 us; the launch traced here: 67.2 us
  Pallas kernels  66.6 us (99%)
    pallas_call x1, Pallas kernels, local(): pl.pallas_call(functools.partial(kernel, n, n_off, slots, float(width * n...  64.9 us
    pallas_call x1, Pallas kernels, local(): pl.pallas_call(hand_over, out_shape=(jax.ShapeDtypeStruct((k, width), f32...  1.67 us

profile of v5, /device:TPU:0, one launch (start us, length us, event | category | flops | bytes accessed | tf_op | source)
XLA Modules:
  0.0 67.2 jit_solution(17475240069282555315)
XLA Ops:
  0.6 64.9 %shard_map.68 = (f32[64,1024]{1,0:T(8,128)}, f32[64,64]{1,0:T(8,128)}) custom-call(f32[64,1024]{1,0:T(8,128)} %vec_hbm.1, f32[1024,2048]{1,0:T(8,128)} %tiles_ref.1, s32[1,2]{1,0:T(1,128)} %live_hbm.1, f32[1,1024]{1,0:T(1,128)} %bitcast.2, f32[1,1024]{1,0:T(1,128)} %bitcast.3), custom_call_target="tpu_custom_call" | custom-call | tf_op jit(solution)/shard_map/pallas_call | solution.py:492
  65.5 1.7 %shard_map.69 = (f32[64,1024]{1,0:T(8,128)}, f32[64,64]{1,0:T(8,128)}) custom-call(f32[64,1024]{1,0:T(8,128)} %get-tuple-element.4.basis_in, f32[64,64]{1,0:T(8,128)} %get-tuple-element.5.ritz_in), custom_call_target="tpu_custom_call" | custom-call | tf_op jit(solution)/shard_map/pallas_call | solution.py:548

commit v6 on v5

--- a/solution.py
+++ b/solution.py
@@ -318,9 +318,11 @@
     put_split(slots, precond_ref[...] * vec_ref[...])
     for slot in order:
         transposed((1,), slot)
+        deliver(1, slot)
     for slot in range(slots):
         put_split(slot, near[slot, k : k + 1, :] * near[slot, :k, :])
         forward((1,), slot, slot == 0)
+    exchange(1)
 
     p_part = precond_ref[:, cols(off)]
 
@@ -343,9 +345,6 @@
             ).start()
         if not last:
             spread(part_a.at[it], near_a, share_send, share_recv, begin)
-            for slot in order:
-                deliver(1, slot)
-            exchange(1)
 
         ab = jnp.concatenate([a_part, p_part * x_part], axis=0)
         inner = triple(ab, ab, NT)

time: 67.3 us -> 68.4 us (1.016)
  Pallas kernels: 66.6 us -> 67.6 us
    pallas_call x1, Pallas kernels: 64.9 us -> 65.9 us  [local(): pl.pallas_call(functools.partial(kernel, n, n_off, slots, float(width * n...]
where the time goes in v6:
time: 68.4 us; the launch traced here: 68.2 us
  Pallas kernels  67.6 us (99%)
    pallas_call x1, Pallas kernels, local(): pl.pallas_call(functools.partial(kernel, n, n_off, slots, float(width * n...  65.9 us
    pallas_call x1, Pallas kernels, local(): pl.pallas_call(hand_over, out_shape=(jax.ShapeDtypeStruct((k, width), f32...  1.67 us

profile of v6, /device:TPU:0, one launch (start us, length us, event | category | flops | bytes accessed | tf_op | source)
XLA Modules:
  0.0 68.2 jit_solution(7669774825969771688)
XLA Ops:
  0.6 65.9 %shard_map.68 = (f32[64,1024]{1,0:T(8,128)}, f32[64,64]{1,0:T(8,128)}) custom-call(f32[64,1024]{1,0:T(8,128)} %vec_hbm.1, f32[1024,2048]{1,0:T(8,128)} %tiles_ref.1, s32[1,2]{1,0:T(1,128)} %live_hbm.1, f32[1,1024]{1,0:T(1,128)} %bitcast.2, f32[1,1024]{1,0:T(1,128)} %bitcast.3), custom_call_target="tpu_custom_call" | custom-call | tf_op jit(solution)/shard_map/pallas_call | solution.py:491
  66.6 1.7 %shard_map.69 = (f32[64,1024]{1,0:T(8,128)}, f32[64,64]{1,0:T(8,128)}) custom-call(f32[64,1024]{1,0:T(8,128)} %get-tuple-element.4.basis_in, f32[64,64]{1,0:T(8,128)} %get-tuple-element.5.ritz_in), custom_call_target="tpu_custom_call" | custom-call | tf_op jit(solution)/shard_map/pallas_call | solution.py:547
